TPU v7x, 256 devices: a whole 4x4x8 slice. The times are simulated.
256 devices in a mesh: gx: 32 (over y, z_lo, core), gy: 8 (over x, z_hi).
Axes of the slice: x: 4, y: 4, z: 8 (z_hi: 2, z_lo: 4; z = z_hi * 4 + z_lo), core: 2. Of those that a mesh axis runs over, the one named last changes fastest.
Arguments:
- phase_fields: float32 [16, 512, 128, 128], P(None, 'gx', 'gy'), may hold values from 0 to 1, as said below
- grain_ids: int32 [32, 8, 8, 16], P('gx', 'gy'), may hold values from -1 to 4095, as said below
Outputs:
- phase_out: float32 [16, 512, 128, 128], P(None, 'gx', 'gy')
Inputs may be any that keep to these rules, and one draw needn't show every extreme that they name: `grain_ids`: A tile lists distinct grains; between 5 * 16 / 8 (rounded down) and 15 slots are active, in random slots; every grain is listed by some tile, and grains of adjacent tiles appear in several tiles. `phase_fields`: the field of an empty slot is zero in the whole tile.
All inputs are finite; a program needn't handle non-finite values.
Results may differ from a plain program's by a relative error of at most 0.0001.
Values sent between devices are 32-bit elements; how exact they have to be, the bound alone decides.
No kernel may reach another device: no remote copies, remote signals or barrier semaphores. Data moves between devices by JAX's collectives and lax.ppermute only.
A program may use at most 256 MiB of HBM per device.

v0:
```python
import jax
import jax.numpy as jnp
from jax import lax
from jax.sharding import PartitionSpec as P

STEPS = 2


TIME_STEP = 0.05
INTERFACE_GAMMA = 1.5
GRADIENT_KAPPA = 0.5


def padded(cells, sides, width):
    for axis, dim in sides:
        count = lax.axis_size(axis)
        head = lax.slice_in_dim(cells, 0, width, axis=dim)
        tail = lax.slice_in_dim(cells, cells.shape[dim] - width, cells.shape[dim], axis=dim)
        cells = jnp.concatenate(
            [
                lax.ppermute(tail, axis, [(i, (i + 1) % count) for i in range(count)]),
                cells,
                lax.ppermute(head, axis, [((i + 1) % count, i) for i in range(count)]),
            ],
            axis=dim,
        )
    return cells


def remap_edge(source, mine, other, axis, step):
    slots, cells_x, cells_y, cells_z = source.shape
    tiles_x, tiles_y, tiles_z, _ = mine.shape
    shaped = source.reshape(
        slots, tiles_x, cells_x // tiles_x, tiles_y, cells_y // tiles_y, tiles_z, cells_z // tiles_z
    )
    edge = shaped.shape[2 * axis] - 1 if step > 0 else 0
    match = ((mine[..., :, None] == other[..., None, :]) & (mine[..., :, None] >= 0)).astype(
        jnp.float32
    )
    plane = lax.index_in_dim(shaped, edge, 2 * axis, keepdims=True)
    moved = jnp.einsum("abcst,taibjck->saibjck", match, plane, precision=lax.Precision.HIGHEST)
    place = lax.broadcasted_iota(jnp.int32, shaped.shape, 2 * axis) == edge
    return jnp.where(place, moved, shaped).reshape(source.shape)


def update(field, parts):
    laplace = parts[0] + parts[1] + (parts[2] + parts[3]) + (parts[4] + parts[5]) - 6.0 * field
    total = jnp.sum(field * field, axis=0)
    square = field * field
    force = (
        square * field
        - field
        + 2.0 * INTERFACE_GAMMA * field * (total - square)
        - GRADIENT_KAPPA * laplace
    )
    return field - TIME_STEP * force


def advance(field, grain_ids, ids_around):
    x_wide = padded(field, (("gx", 1),), 1)
    y_wide = padded(field, (("gy", 2),), 1)
    parts = [
        remap_edge(x_wide[:, :-2], grain_ids, ids_around[0:1, 1:2], 1, -1),
        remap_edge(x_wide[:, 2:], grain_ids, ids_around[2:3, 1:2], 1, 1),
        remap_edge(y_wide[:, :, :-2], grain_ids, ids_around[1:2, 0:1], 2, -1),
        remap_edge(y_wide[:, :, 2:], grain_ids, ids_around[1:2, 2:3], 2, 1),
    ]
    for step in (-1, 1):
        source = jnp.roll(field, -step, 3)
        other = jnp.roll(grain_ids, -step, 2)
        parts.append(remap_edge(source, grain_ids, other, 3, step))
    return update(field, parts)


def shards(phase_fields, grain_ids):
    ids_around = padded(grain_ids, (("gx", 0), ("gy", 1)), 1)
    field = phase_fields
    for turn in range(STEPS):
        field = advance(field, grain_ids, ids_around)
    return field


def solution(mesh):
    in_specs = (P(None, "gx", "gy", None), P("gx", "gy", None, None))
    out_specs = P(None, "gx", "gy", None)
    return jax.shard_map(shards, mesh=mesh, in_specs=in_specs, out_specs=out_specs, check_vma=False)
```

profile of v0, /device:TPU:0, one launch (start us, length us, event | category | flops | bytes accessed | tf_op | source)
XLA Modules:
  0.0 483.2 jit_solution(7784019061040345390)
XLA Ops:
  0.0 5.7 %collective-permute-start.3 = (s32[1,1,8,16]{3,2,1,0:T(8,128)}, s32[1,1,8,16]{3,2,1,0:T(8,128)}, u32[]{:S(2)}, u32[]{:S(2)}) collective-permute-start(s32[1,1,8,16]{3,2,1,0:T(8,128)} %param.3), channel_id=1, source_target_pairs={{8,0},{16,8},{24,16},{32,24},{40,32},{48,40},{56,48},{64,56},{72,6... | collective-permute-start | bytes 1544 | tf_op jit(solution)/shard_map/ppermute | solution.py:23
  5.7 2.4 fusion.76
  8.1 7.6 %collective-permute-start.6 = (f32[16,16,1,128]{3,1,2,0:T(8,128)}, f32[16,16,1,128]{3,1,2,0:T(8,128)S(1)}, u32[]{:S(2)}, u32[]{:S(2)}) collective-permute-start(f32[16,16,1,128]{3,1,2,0:T(8,128)} %bitcast.88), channel_id=1, source_target_pairs={{1,0},{2,1},{3,2},{4,3},{5,4},{6,5},{7,6},{0,7},{9,8},{10,9},{11,1... | collective-permute-start | bytes 393224 | tf_op jit(solution)/shard_map/ppermute | solution.py:23
  15.7 1.7 fusion.75
  17.5 5.8 %collective-permute-start.2 = (f32[16,1,16,128]{3,2,1,0:T(8,128)}, f32[16,1,16,128]{3,2,1,0:T(8,128)S(1)}, u32[]{:S(2)}, u32[]{:S(2)}) collective-permute-start(f32[16,1,16,128]{3,2,1,0:T(8,128)} %get-tuple-element.25), channel_id=1, source_target_pairs={{8,0},{16,8},{24,16},{32,24},{40,32},{48,40},{56,48},{64,56},{72,6... | collective-permute-start | bytes 393224 | tf_op jit(solution)/shard_map/ppermute | solution.py:23
  23.3 3.0 fusion.78
  28.2 3.2 pad_maximum_fusion.8
  31.4 10.6 %reshape.246 = f32[16,1,16,1,16,8,16]{6,5,4,2,0,3,1:T(8,128)} reshape(f32[16,16,16,128]{3,2,1,0:T(8,128)} %get-tuple-element.37) | data formatting | bytes 4194304 | tf_op jit(solution)/shard_map/reshape | solution.py:33
  42.0 12.8 %slice.197 = f32[16,1,16,1,16,8,1]{6,5,4,2,0,3,1:T(8,128)} slice(f32[16,1,16,1,16,8,16]{6,5,4,2,0,3,1:T(8,128)} %reshape.246), slice={[0:16], [0:1], [0:16], [0:1], [0:16], [0:8], [15:16]} | slice | bytes 262144 | tf_op jit(solution)/shard_map/slice | solution.py:40
  54.8 14.2 %copy.132 = f32[16,1,16,1,16,8,1]{0,4,2,5,6,3,1:T(8,128)S(1)} copy(f32[16,1,16,1,16,8,1]{6,5,4,2,0,3,1:T(8,128)} %slice.197) | data formatting | bytes 262144
  69.0 10.6 %reshape.244 = f32[16,1,16,1,16,8,16]{6,5,4,2,0,3,1:T(8,128)} reshape(f32[16,16,16,128]{3,2,1,0:T(8,128)} %get-tuple-element.36) | data formatting | bytes 4194304 | tf_op jit(solution)/shard_map/reshape | solution.py:33
  79.6 15.1 %copy.131 = f32[16,1,16,1,16,8,1]{0,4,2,5,6,3,1:T(8,128)} copy(f32[16,1,16,1,16,8,1]{6,5,4,2,0,3,1:T(8,128)} %bitcast.221) | data formatting | bytes 262144
  95.4 1.6 convolution_bitcast_fusion.6
  101.0 8.3 %collective-permute-start.7 = (s32[3,1,8,16]{3,2,1,0:T(8,128)}, s32[3,1,8,16]{3,2,1,0:T(8,128)}, u32[]{:S(2)}, u32[]{:S(2)}) collective-permute-start(s32[3,1,8,16]{3,2,1,0:T(8,128)} %constant_dynamic-update-slice_fusion), channel_id=1, source_target_pairs={{1,0},{2,1},{3,2},{4,3},{5,4},{6,5},{7,6},{0,7},{9,8},{10,9},{11,1... | collective-permute-start | bytes 4616 | tf_op jit(solution)/shard_map/ppermute | solution.py:23
  109.8 4.1 copy.102
  113.8 9.9 %broadcast_in_dim.151 = f32[16,16,16,8,16]{4,3,2,1,0:T(8,128)} broadcast(f32[16,16,16,8]{3,2,1,0:T(8,128)} %copy.102), dimensions={0,1,2,3} | broadcast | bytes 2228224 | tf_op jit(solution)/shard_map/jit(_where)/broadcast_in_dim | solution.py:43
  123.7 11.4 %broadcast_in_dim.152 = f32[16,16,16,128]{3,2,1,0:T(8,128)} reshape(f32[16,16,16,8,16]{4,3,2,1,0:T(8,128)} %broadcast_in_dim.151) | data formatting | bytes 4194304 | tf_op jit(solution)/shard_map/jit(_where)/broadcast_in_dim | solution.py:43
  137.6 2.9 copy.100
  140.5 9.9 %broadcast_in_dim.148 = f32[16,16,16,8,16]{4,3,2,1,0:T(8,128)} broadcast(f32[16,16,16,8]{3,2,1,0:T(8,128)} %copy.100), dimensions={0,1,2,3} | broadcast | bytes 2228224 | tf_op jit(solution)/shard_map/jit(_where)/broadcast_in_dim | solution.py:43
  150.4 11.4 %broadcast_in_dim.149 = f32[16,16,16,128]{3,2,1,0:T(8,128)} reshape(f32[16,16,16,8,16]{4,3,2,1,0:T(8,128)} %broadcast_in_dim.148) | data formatting | bytes 4194304 | tf_op jit(solution)/shard_map/jit(_where)/broadcast_in_dim | solution.py:43
  163.1 9.2 %collective-permute-done.5 = s32[3,1,8,16]{3,2,1,0:T(8,128)S(1)} collective-permute-done((s32[3,1,8,16]{3,2,1,0:T(8,128)}, s32[3,1,8,16]{3,2,1,0:T(8,128)S(1)}, u32[]{:S(2)}, u32[]{:S(2)}) %collective-permute-start.5) | collective-permute-done | bytes 1568 | tf_op jit(solution)/shard_map/ppermute | solution.py:21
  173.0 5.2 %multiply_reduce_fusion.1 = (f32[16,16,128]{2,1,0:T(8,128)}, f32[16,16,16,128]{3,2,1,0:T(8,128)}, f32[16,16,16,128]{3,2,1,0:T(8,128)}, f32[16,16,16,128]{3,2,1,0:T(8,128)}, f32[16,16,16,128]{3,2,1,0:T(8,128)}) fusion(f32[16,16,16,128]{3,2,1,0:T(8,128)S(1)} %copy-done, f32[16,1,16,128]{3,2,1,0:T(8,128)S(1)} %collective-permute-done, ...), kind=kLoop, calls=%fused_computation.5 | loop fusion | flops 3112960 | bytes 11141120 | tf_op jit(solution)/shard_map/reduce_sum | solution.py:48
  178.2 11.0 %reshape.242 = f32[16,1,16,1,16,8,16]{6,5,4,2,0,3,1:T(8,128)} reshape(f32[16,16,16,128]{3,2,1,0:T(8,128)} %get-tuple-element.23) | data formatting | bytes 4194304 | tf_op jit(solution)/shard_map/reshape | solution.py:33
  192.7 2.3 copy.98
  195.9 8.4 %reshape.240 = f32[16,1,16,1,16,8,16]{6,5,4,2,0,3,1:T(8,128)} reshape(f32[16,16,16,128]{3,2,1,0:T(8,128)S(1)} %copy-done.6) | data formatting | bytes 4194304 | tf_op jit(solution)/shard_map/reshape | solution.py:33
  207.8 2.3 copy.94
  211.0 8.4 %reshape.238 = f32[16,1,16,1,16,8,16]{6,5,4,2,0,3,1:T(8,128)} reshape(f32[16,16,16,128]{3,2,1,0:T(8,128)S(1)} %copy-done.5) | data formatting | bytes 4194304 | tf_op jit(solution)/shard_map/reshape | solution.py:33
  221.3 2.3 convolution_bitcast_fusion.10
  223.6 2.3 copy.90
  226.8 8.4 %reshape.236 = f32[16,1,16,1,16,8,16]{6,5,4,2,0,3,1:T(8,128)} reshape(f32[16,16,16,128]{3,2,1,0:T(8,128)S(1)} %copy-done.4) | data formatting | bytes 4194304 | tf_op jit(solution)/shard_map/reshape | solution.py:33
  239.6 10.3 %multiply_reduce_fusion = (f32[16,16,128]{2,1,0:T(8,128)}, f32[16,16,16,128]{3,2,1,0:T(8,128)S(1)}) fusion(f32[16,16,16,128]{3,2,1,0:T(8,128)} %param.2, f32[16,16,16,128]{3,2,1,0:T(8,128)} %broadcast_in_dim.152, f32[16,16,16,128]{3,2,1,0:T(8,128)} %get-tuple-element.37, pred[128]{0:T(512)(128)(4,1)} %iota.98, f32[16,16,16,128]{3,2,1,0:T(8,128)} %broadcast_in_dim.149, ...), kind=kLoop, calls=%fused_computation.3 | loop fusion | flops 15695872 | bytes 13893920 | tf_op jit(solution)/shard_map/reduce_sum | solution.py:48
  249.9 2.1 fusion.73
  252.0 2.1 fusion.74
  255.8 1.9 pad_maximum_fusion.11
  257.7 10.6 %reshape.258 = f32[16,1,16,1,16,8,16]{6,5,4,2,0,3,1:T(8,128)} reshape(f32[16,16,16,128]{3,2,1,0:T(8,128)} %pad_maximum_fusion.11) | data formatting | bytes 4194304 | tf_op jit(solution)/shard_map/reshape | solution.py:33
  268.3 12.8 %slice.211 = f32[16,1,16,1,16,8,1]{6,5,4,2,0,3,1:T(8,128)} slice(f32[16,1,16,1,16,8,16]{6,5,4,2,0,3,1:T(8,128)} %reshape.258), slice={[0:16], [0:1], [0:16], [0:1], [0:16], [0:8], [15:16]} | slice | bytes 262144 | tf_op jit(solution)/shard_map/slice | solution.py:40
  281.1 15.0 %copy.138 = f32[16,1,16,1,16,8,1]{0,4,2,5,6,3,1:T(8,128)} copy(f32[16,1,16,1,16,8,1]{6,5,4,2,0,3,1:T(8,128)} %slice.211) | data formatting | bytes 262144
  296.2 2.0 convolution_bitcast_fusion
  298.2 3.6 pad_maximum_fusion.10
  301.8 10.6 %reshape.256 = f32[16,1,16,1,16,8,16]{6,5,4,2,0,3,1:T(8,128)} reshape(f32[16,16,16,128]{3,2,1,0:T(8,128)} %pad_maximum_fusion.10) | data formatting | bytes 4194304 | tf_op jit(solution)/shard_map/reshape | solution.py:33
  312.3 15.0 %copy.137 = f32[16,1,16,1,16,8,1]{0,4,2,5,6,3,1:T(8,128)} copy(f32[16,1,16,1,16,8,1]{6,5,4,2,0,3,1:T(8,128)} %bitcast.220) | data formatting | bytes 262144
  327.4 5.7 %collective-permute-start.9 = (f32[16,1,16,128]{3,2,1,0:T(8,128)}, f32[16,1,16,128]{3,2,1,0:T(8,128)S(1)}, u32[]{:S(2)}, u32[]{:S(2)}) collective-permute-start(f32[16,1,16,128]{3,2,1,0:T(8,128)} %get-tuple-element.12), channel_id=1, source_target_pairs={{8,0},{16,8},{24,16},{32,24},{40,32},{48,40},{56,48},{64,56},{72,6... | collective-permute-start | bytes 393224 | tf_op jit(solution)/shard_map/ppermute | solution.py:23
  333.0 8.0 %collective-permute-start.11 = (f32[16,16,1,128]{3,1,2,0:T(8,128)}, f32[16,16,1,128]{3,1,2,0:T(8,128)}, u32[]{:S(2)}, u32[]{:S(2)}) collective-permute-start(f32[16,16,1,128]{3,1,2,0:T(8,128)} %bitcast.236), channel_id=1, source_target_pairs={{1,0},{2,1},{3,2},{4,3},{5,4},{6,5},{7,6},{0,7},{9,8},{10,9},{11,1... | collective-permute-start | bytes 393224 | tf_op jit(solution)/shard_map/ppermute | solution.py:23
  341.1 2.9 convolution_bitcast_fusion.1
  344.0 2.9 copy.118
  346.8 10.1 %broadcast_in_dim.165 = f32[16,16,16,8,16]{4,3,2,1,0:T(8,128)} broadcast(f32[16,16,16,8]{3,2,1,0:T(8,128)} %copy.118), dimensions={0,1,2,3} | broadcast | bytes 2228224 | tf_op jit(solution)/shard_map/jit(_where)/broadcast_in_dim | solution.py:43
  356.9 11.5 %broadcast_in_dim.166 = f32[16,16,16,128]{3,2,1,0:T(8,128)} reshape(f32[16,16,16,8,16]{4,3,2,1,0:T(8,128)} %broadcast_in_dim.165) | data formatting | bytes 4194304 | tf_op jit(solution)/shard_map/jit(_where)/broadcast_in_dim | solution.py:43
  368.5 2.9 copy.116
  371.3 9.9 %broadcast_in_dim.162 = f32[16,16,16,8,16]{4,3,2,1,0:T(8,128)} broadcast(f32[16,16,16,8]{3,2,1,0:T(8,128)} %copy.116), dimensions={0,1,2,3} | broadcast | bytes 2228224 | tf_op jit(solution)/shard_map/jit(_where)/broadcast_in_dim | solution.py:43
  381.2 11.4 %broadcast_in_dim.163 = f32[16,16,16,128]{3,2,1,0:T(8,128)} reshape(f32[16,16,16,8,16]{4,3,2,1,0:T(8,128)} %broadcast_in_dim.162) | data formatting | bytes 4194304 | tf_op jit(solution)/shard_map/jit(_where)/broadcast_in_dim | solution.py:43
  392.7 4.6 pad_maximum_fusion.3
  397.3 10.6 %reshape.254 = f32[16,1,16,1,16,8,16]{6,5,4,2,0,3,1:T(8,128)} reshape(f32[16,16,16,128]{3,2,1,0:T(8,128)} %get-tuple-element.10) | data formatting | bytes 4194304 | tf_op jit(solution)/shard_map/reshape | solution.py:33
  410.7 2.8 convolution_bitcast_fusion.2
  413.5 2.1 copy.114
  416.6 10.6 %reshape.252 = f32[16,1,16,1,16,8,16]{6,5,4,2,0,3,1:T(8,128)} reshape(f32[16,16,16,128]{3,2,1,0:T(8,128)} %get-tuple-element.9) | data formatting | bytes 4194304 | tf_op jit(solution)/shard_map/reshape | solution.py:33
  430.0 2.9 convolution_bitcast_fusion.3
  432.9 2.1 copy.110
  436.0 10.8 %reshape.250 = f32[16,1,16,1,16,8,16]{6,5,4,2,0,3,1:T(8,128)} reshape(f32[16,16,16,128]{3,2,1,0:T(8,128)} %get-tuple-element.8) | data formatting | bytes 4194304 | tf_op jit(solution)/shard_map/reshape | solution.py:33
  449.6 2.9 convolution_bitcast_fusion.4
  452.5 2.1 copy.106
  455.5 10.6 %reshape.248 = f32[16,1,16,1,16,8,16]{6,5,4,2,0,3,1:T(8,128)} reshape(f32[16,16,16,128]{3,2,1,0:T(8,128)} %get-tuple-element.7) | data formatting | bytes 4194304 | tf_op jit(solution)/shard_map/reshape | solution.py:33
  468.9 2.9 convolution_bitcast_fusion.5
  471.8 2.1 copy.104
  474.9 7.8 %fusion.9 = f32[16,16,16,128]{3,2,1,0:T(8,128)} fusion(f32[16,16,16,128]{3,2,1,0:T(8,128)S(1)} %get-tuple-element.6, f32[16,16,16,128]{3,2,1,0:T(8,128)} %broadcast_in_dim.166, f32[16,16,16,128]{3,2,1,0:T(8,128)} %broadcast_in_dim.163, f32[16,16,128]{2,1,0:T(8,128)} %broadcast_in_dim.159, f32[16,16,128]{2,1,0:T(8,128)} %broadcast_in_dim.157, ...), kind=kLoop, calls=%fused_computation.15 | loop fusion | flops 15728640 | bytes 13762848 | tf_op jit(solution)/shard_map/sub | solution.py:56
  (111 shorter events, 44.2 us)
Async XLA Ops:
  0.0 97.7 %collective-permute-start.1 = (s32[1,1,8,16]{3,2,1,0:T(8,128)}, s32[1,1,8,16]{3,2,1,0:T(8,128)}, u32[]{:S(2)}, u32[]{:S(2)}) collective-permute-start(s32[1,1,8,16]{3,2,1,0:T(8,128)} %param.3), channel_id=1, source_target_pairs={{0,8},{8,16},{16,24},{24,32},{32,40},{40,48},{48,56},{56,64},{64,7... | collective-permute-start | bytes 1544 | tf_op jit(solution)/shard_map/ppermute | solution.py:21
  0.0 99.7 %collective-permute-start.3 = (s32[1,1,8,16]{3,2,1,0:T(8,128)}, s32[1,1,8,16]{3,2,1,0:T(8,128)}, u32[]{:S(2)}, u32[]{:S(2)}) collective-permute-start(s32[1,1,8,16]{3,2,1,0:T(8,128)} %param.3), channel_id=1, source_target_pairs={{8,0},{16,8},{24,16},{32,24},{40,32},{48,40},{56,48},{64,56},{72,6... | collective-permute-start | bytes 1544 | tf_op jit(solution)/shard_map/ppermute | solution.py:23
  8.1 164.9 %collective-permute-start.6 = (f32[16,16,1,128]{3,1,2,0:T(8,128)}, f32[16,16,1,128]{3,1,2,0:T(8,128)S(1)}, u32[]{:S(2)}, u32[]{:S(2)}) collective-permute-start(f32[16,16,1,128]{3,1,2,0:T(8,128)} %bitcast.88), channel_id=1, source_target_pairs={{1,0},{2,1},{3,2},{4,3},{5,4},{6,5},{7,6},{0,7},{9,8},{10,9},{11,1... | collective-permute-start | bytes 393224 | tf_op jit(solution)/shard_map/ppermute | solution.py:23
  17.4 155.5 %collective-permute-start = (f32[16,1,16,128]{3,2,1,0:T(8,128)}, f32[16,1,16,128]{3,2,1,0:T(8,128)S(1)}, u32[]{:S(2)}, u32[]{:S(2)}) collective-permute-start(f32[16,1,16,128]{3,2,1,0:T(8,128)} %get-tuple-element.24), channel_id=1, source_target_pairs={{0,8},{8,16},{16,24},{24,32},{32,40},{40,48},{48,56},{56,64},{64,7... | collective-permute-start | bytes 393224 | tf_op jit(solution)/shard_map/ppermute | solution.py:21
  17.4 8.8 %copy-start = (f32[16,16,16,128]{3,2,1,0:T(8,128)S(1)}, f32[16,16,16,128]{3,2,1,0:T(8,128)}, u32[]{:S(2)}) copy-start(f32[16,16,16,128]{3,2,1,0:T(8,128)} %param.2) | copy-start | bytes 6291460
  17.5 155.5 %collective-permute-start.2 = (f32[16,1,16,128]{3,2,1,0:T(8,128)}, f32[16,1,16,128]{3,2,1,0:T(8,128)S(1)}, u32[]{:S(2)}, u32[]{:S(2)}) collective-permute-start(f32[16,1,16,128]{3,2,1,0:T(8,128)} %get-tuple-element.25), channel_id=1, source_target_pairs={{8,0},{16,8},{24,16},{32,24},{40,32},{48,40},{56,48},{64,56},{72,6... | collective-permute-start | bytes 393224 | tf_op jit(solution)/shard_map/ppermute | solution.py:23
  26.3 0.8 copy-start.9
  94.7 2.4 copy-start.7
  97.7 75.3 %collective-permute-start.4 = (f32[16,16,1,128]{3,1,2,0:T(8,128)}, f32[16,16,1,128]{3,1,2,0:T(8,128)}, u32[]{:S(2)}, u32[]{:S(2)}) collective-permute-start(f32[16,16,1,128]{3,1,2,0:T(8,128)} %bitcast.87), channel_id=1, source_target_pairs={{0,1},{1,2},{2,3},{3,4},{4,5},{5,6},{6,7},{7,0},{8,9},{9,10},{10,1... | collective-permute-start | bytes 393224 | tf_op jit(solution)/shard_map/ppermute | solution.py:21
  101.0 61.5 %collective-permute-start.7 = (s32[3,1,8,16]{3,2,1,0:T(8,128)}, s32[3,1,8,16]{3,2,1,0:T(8,128)}, u32[]{:S(2)}, u32[]{:S(2)}) collective-permute-start(s32[3,1,8,16]{3,2,1,0:T(8,128)} %constant_dynamic-update-slice_fusion), channel_id=1, source_target_pairs={{1,0},{2,1},{3,2},{4,3},{5,4},{6,5},{7,6},{0,7},{9,8},{10,9},{11,1... | collective-permute-start | bytes 4616 | tf_op jit(solution)/shard_map/ppermute | solution.py:23
  150.4 11.4 %copy-start.16 = (pred[16]{0:T(512)(128)(4,1)S(1)}, pred[16]{0:T(512)(128)(4,1)}, u32[]{:S(2)}) copy-start(pred[16]{0:T(512)(128)(4,1)} %get-tuple-element.41) | copy-start | bytes 52
  162.5 9.9 %collective-permute-start.5 = (s32[3,1,8,16]{3,2,1,0:T(8,128)}, s32[3,1,8,16]{3,2,1,0:T(8,128)S(1)}, u32[]{:S(2)}, u32[]{:S(2)}) collective-permute-start(s32[3,1,8,16]{3,2,1,0:T(8,128)} %constant_dynamic-update-slice_fusion), channel_id=1, source_target_pairs={{0,1},{1,2},{2,3},{3,4},{4,5},{5,6},{6,7},{7,0},{8,9},{9,10},{10,1... | collective-permute-start | bytes 4616 | tf_op jit(solution)/shard_map/ppermute | solution.py:21
  163.1 27.9 %copy-start.13 = (s32[8,16]{1,0:T(8,128)}, s32[8,16]{1,0:T(8,128)S(1)}, u32[]{:S(2)}) copy-start(s32[8,16]{1,0:T(8,128)S(1)} %slice_bitcast_fusion) | copy-start | bytes 1540
  189.2 1.2 slice-start
  192.7 3.2 copy-start.6
  204.3 1.2 slice-start.1
  204.3 1.8 copy-start.11
  207.8 3.2 copy-start.5
  219.5 1.2 slice-start.2
  223.6 3.2 copy-start.4
  235.3 1.2 slice-start.3
  252.0 3.8 copy-start.2
  254.1 1.7 copy-start.3
  296.2 2.0 copy-start.1
  327.4 65.3 %collective-permute-start.8 = (f32[16,1,16,128]{3,2,1,0:T(8,128)}, f32[16,1,16,128]{3,2,1,0:T(8,128)S(1)}, u32[]{:S(2)}, u32[]{:S(2)}) collective-permute-start(f32[16,1,16,128]{3,2,1,0:T(8,128)} %get-tuple-element.11), channel_id=1, source_target_pairs={{0,8},{8,16},{16,24},{24,32},{32,40},{40,48},{48,56},{56,64},{64,7... | collective-permute-start | bytes 393224 | tf_op jit(solution)/shard_map/ppermute | solution.py:21
  327.4 65.3 %collective-permute-start.9 = (f32[16,1,16,128]{3,2,1,0:T(8,128)}, f32[16,1,16,128]{3,2,1,0:T(8,128)S(1)}, u32[]{:S(2)}, u32[]{:S(2)}) collective-permute-start(f32[16,1,16,128]{3,2,1,0:T(8,128)} %get-tuple-element.12), channel_id=1, source_target_pairs={{8,0},{16,8},{24,16},{32,24},{40,32},{48,40},{56,48},{64,56},{72,6... | collective-permute-start | bytes 393224 | tf_op jit(solution)/shard_map/ppermute | solution.py:23
  333.0 59.6 %collective-permute-start.10 = (f32[16,16,1,128]{3,1,2,0:T(8,128)}, f32[16,16,1,128]{3,1,2,0:T(8,128)}, u32[]{:S(2)}, u32[]{:S(2)}) collective-permute-start(f32[16,16,1,128]{3,1,2,0:T(8,128)} %bitcast.237), channel_id=1, source_target_pairs={{0,1},{1,2},{2,3},{3,4},{4,5},{5,6},{6,7},{7,0},{8,9},{9,10},{10,1... | collective-permute-start | bytes 393224 | tf_op jit(solution)/shard_map/ppermute | solution.py:21
  333.0 59.6 %collective-permute-start.11 = (f32[16,16,1,128]{3,1,2,0:T(8,128)}, f32[16,16,1,128]{3,1,2,0:T(8,128)}, u32[]{:S(2)}, u32[]{:S(2)}) collective-permute-start(f32[16,16,1,128]{3,1,2,0:T(8,128)} %bitcast.236), channel_id=1, source_target_pairs={{1,0},{2,1},{3,2},{4,3},{5,4},{6,5},{7,6},{0,7},{9,8},{10,9},{11,1... | collective-permute-start | bytes 393224 | tf_op jit(solution)/shard_map/ppermute | solution.py:23
  356.9 11.5 %copy-start.8 = (f32[16,16,16,8]{0,2,1,3:T(8,128)S(1)}, f32[16,16,16,8]{0,2,1,3:T(8,128)}, u32[]{:S(2)}) copy-start(f32[16,16,16,8]{0,2,1,3:T(8,128)} %convolution_bitcast_fusion.1) | copy-start | bytes 393220
  407.9 1.2 slice-start.4
  407.9 2.8 copy-start.14
  427.2 1.2 slice-start.5
  427.2 2.8 copy-start.12
  446.8 1.2 slice-start.6
  466.1 1.2 slice-start.7
  471.8 3.1 copy-start.10
  471.8 3.1 copy-start.15
  471.8 3.1 copy-start.17
  471.8 3.1 copy-start.18
  471.8 3.1 copy-start.19
where the time goes:
time: 491 us; the launch traced here: 483 us
  local copies, waits for them, and re-layouts  368 us (75%)
  starting transfers between devices  41.2 us (8%)
  other arithmetic  38 us (8%)
  matrix products  25.6 us (5%)
  waiting for transfers between devices  9.27 us (2%)
    reshape x12, local copies, waits for them, and re-layouts, remap_edge(): source.reshape(slots, tiles_x, cells_x // tiles_x, tiles_y, cells_y // ti...  121 us
    broadcast_in_dim x20, local copies, waits for them, and re-layouts, remap_edge(): return jnp.where(place, moved, shaped).reshape(source.shape)  105 us
    unnamed x54, local copies, waits for them, and re-layouts  70 us
    ppermute x6, starting transfers between devices, padded(): lax.ppermute(head, axis, [((i + 1) % count, i) for i in range(count)])  41.1 us
    slice x18, local copies, waits for them, and re-layouts, remap_edge(): plane = lax.index_in_dim(shaped, edge, 2 * axis, keepdims=True)  35.4 us
    dot_general x12, matrix products, remap_edge(): jnp.einsum('abcst,taibjck->saibjck', match, plane, precision=lax.Precisio...  25.6 us
    transpose x8, local copies, waits for them, and re-layouts, remap_edge(): jnp.einsum('abcst,taibjck->saibjck', match, plane, precision=lax.Precisio...  16.1 us
    reduce_sum x2, other arithmetic, update(): total = jnp.sum(field * field, axis=0)  15.5 us
  transfers between devices with their start and end apart: 12, of which 1 were waited for; matrix products, arithmetic and copies ran while one was open for 39% of the time, Pallas kernels for 0%

commit v1 on v0

v1 whole, which is shorter than its diff:
```python
import jax
import jax.numpy as jnp
from jax import lax
from jax.experimental import pallas as pl
from jax.experimental.pallas import tpu as pltpu
from jax.sharding import PartitionSpec as P

SLOTS = 16
TILE = 16
ROWS = TILE * TILE
NZ = 128
NTZ = NZ // TILE
FACE = SLOTS * TILE
HEAD = FACE + 8
RATE = 0.025
HIGHEST = lax.Precision.HIGHEST
F32 = jnp.float32
BF16 = jnp.bfloat16


def iota(shape, dim):
    return lax.broadcasted_iota(jnp.int32, shape, dim)


def sides(axis):
    odd = lax.axis_index(axis) & 1
    return (TILE - 1) * (1 - odd), (TILE - 1) * odd


def flat_ids(ids):
    lane = iota((SLOTS, NZ), 1)
    spread = ((lane & 15) == iota((SLOTS, NZ), 0)).astype(F32)
    wide = jnp.dot(ids.astype(F32), spread, precision=HIGHEST, preferred_element_type=F32)
    own = (iota((NTZ, NZ), 1) >> 4) == iota((NTZ, NZ), 0)
    return jnp.sum(jnp.where(own, wide, 0.0), axis=0, keepdims=True)


def lane_ids(flat):
    pick = jnp.where((iota((SLOTS, NZ), 1) & 15) == iota((SLOTS, NZ), 0), flat, 0.0)
    group = ((iota((NZ, NZ), 0) >> 4) == (iota((NZ, NZ), 1) >> 4)).astype(F32)
    return jnp.dot(pick, group, precision=HIGHEST, preferred_element_type=F32)


def remap(mine, other, plane, match_ref, out_ref, own_ref=None):
    for s in range(SLOTS):
        row = mine[s : s + 1, :]
        match_ref[s] = jnp.where((other == row) & (row >= 0.0), RATE, 0.0)
    for s in range(SLOTS):
        total = None
        if own_ref is not None:
            listed = RATE * jnp.sum(match_ref[s], axis=0, keepdims=True)
            total = listed * own_ref[s * TILE : (s + 1) * TILE, :]
        for t in range(SLOTS):
            term = match_ref[s, t : t + 1, :] * plane[t * TILE : (t + 1) * TILE, :]
            total = term if total is None else total + term
        out_ref[s * TILE : (s + 1) * TILE, :] = total


def take_x(field_ref, x):
    return field_ref[:, pl.ds(pl.multiple_of(x * TILE, TILE), TILE), :].reshape(FACE, NZ)


def take_y(field_ref, s, y):
    return field_ref[s, pl.ds(y, TILE, stride=TILE), :]


def add_faces(field_ref, x_faces, y_faces, xs, ys):
    for ref, x in zip(x_faces, xs):
        at = pl.ds(pl.multiple_of(x * TILE, TILE), TILE)
        field_ref[:, at, :] += ref[...].reshape(SLOTS, TILE, NZ)
    for ref, y in zip(y_faces, ys):
        for s in range(SLOTS):
            at = pl.ds(y, TILE, stride=TILE)
            field_ref[s, at, :] += ref[s * TILE : (s + 1) * TILE, :]


def step(field_ref, ids, out_ref, halves_ref, edge_ref):
    flat = flat_ids(ids)
    mine = lane_ids(flat)
    for s in range(SLOTS):
        value = field_ref[s]
        high = value.astype(BF16)
        halves_ref[s, :, :NZ] = high
        halves_ref[s, :, NZ:] = (value - high.astype(F32)).astype(BF16)
    z, n = iota((2 * NZ, 2 * NZ), 0) & (NZ - 1), iota((2 * NZ, 2 * NZ), 1)
    source = ((n & (NZ - 1)) >> 4) * TILE + jnp.where(n < NZ, TILE - 1, 0)
    at = z == source
    edges = jnp.zeros((ROWS, 2 * NZ), F32)
    for t in range(SLOTS):
        pick = jnp.where(at & ((n & 15) == t), 1.0, 0.0).astype(BF16)
        edges += jnp.dot(halves_ref[t], pick, preferred_element_type=F32)
    high = edges.astype(BF16)
    edge_ref[:, : 2 * NZ] = high
    edge_ref[:, 2 * NZ :] = (edges - high.astype(F32)).astype(BF16)
    r, c = iota((ROWS, ROWS), 0), iota((ROWS, ROWS), 1)
    gap = jnp.abs(r - c)
    beside = (gap == TILE) | ((gap == 1) & ((r >> 4) == (c >> 4)))
    beside = jnp.where(beside, 1.0, 0.0).astype(BF16)
    r, c = iota((2 * NZ, NZ), 0), iota((2 * NZ, NZ), 1)
    rz = r & (NZ - 1)
    along = jnp.where((jnp.abs(rz - c) == 1) & ((rz >> 4) == (c >> 4)), 1.0, 0.0).astype(BF16)
    tile = rz >> 4
    goes = jnp.where(r < NZ, ((tile + 1) & 7) * TILE, ((tile + 7) & 7) * TILE + TILE - 1) == c
    eye = iota((NZ, NZ), 0) == iota((NZ, NZ), 1)
    column = jnp.sum(jnp.where(eye, flat, 0.0), axis=1, keepdims=True)
    column = jnp.concatenate([column, column], axis=0)
    goes = goes & (column >= 0.0)
    total = field_ref[0] * field_ref[0]
    for s in range(1, SLOTS):
        total += field_ref[s] * field_ref[s]
    base = 0.9 - 0.15 * total
    for s in range(SLOTS):
        match = jnp.where(goes & (column == mine[s : s + 1, :]), 1.0, 0.0).astype(BF16)
        near = jnp.dot(halves_ref[s], along, preferred_element_type=F32)
        near += jnp.dot(
            edge_ref[...], jnp.concatenate([match, match], axis=0), preferred_element_type=F32
        )
        plane = jnp.dot(beside, halves_ref[s], preferred_element_type=F32)
        near += plane[:, :NZ] + plane[:, NZ:]
        value = field_ref[s]
        out_ref[s] = value * (base + 0.1 * (value * value)) + RATE * near


def pack_kernel(field_ref, ids_ref, ya_ref, yb_ref, xa_ref, xb_ref):
    flat = flat_ids(ids_ref[...])
    for refs, axis in (((ya_ref, yb_ref), "gy"), ((xa_ref, xb_ref), "gx")):
        for ref, side in zip(refs, sides(axis)):
            if axis == "gx":
                ref[:FACE, :] = take_x(field_ref, side)
            else:
                for s in range(SLOTS):
                    ref[s * TILE : (s + 1) * TILE, :] = take_y(field_ref, s, side)
            ref[FACE:, :] = jnp.broadcast_to(flat, (HEAD - FACE, NZ))


def first_kernel(field_ref, ids_ref, out_ref, ya_ref, yb_ref, xa_ref, xb_ref, halves_ref, edge_ref):
    step(field_ref, ids_ref[...], out_ref, halves_ref, edge_ref)
    for ref, side in zip((xa_ref, xb_ref), sides("gx")):
        ref[...] = take_x(out_ref, side)
    for ref, side in zip((ya_ref, yb_ref), sides("gy")):
        for s in range(SLOTS):
            ref[s * TILE : (s + 1) * TILE, :] = take_y(out_ref, s, side)


def add_corners(out_refs, out_sides, add_refs, add_sides):
    for out_ref, here in zip(out_refs, out_sides):
        for add_ref, there in zip(add_refs, add_sides):
            at = pl.ds(there, SLOTS, stride=TILE)
            out_ref[at, :] += add_ref[pl.ds(here, SLOTS, stride=TILE), :]


def x_kernel(ids_ref, ga_ref, gb_ref, ya_ref, yb_ref, ya_out, yb_out, ca_ref, cb_ref, match_ref):
    mine = lane_ids(flat_ids(ids_ref[...]))
    for got, out in ((ga_ref, ca_ref), (gb_ref, cb_ref)):
        remap(mine, lane_ids(got[FACE : FACE + 1, :]), got, match_ref, out)
    ya_out[...] = ya_ref[...]
    yb_out[...] = yb_ref[...]
    add_corners((ya_out, yb_out), sides("gy"), (ca_ref, cb_ref), sides("gx"))


def y_kernel(ids_ref, ga_ref, gb_ref, xa_ref, xb_ref, cxa_ref, cxb_ref, xa_out, xb_out, ca_ref, cb_ref, match_ref):
    mine = lane_ids(flat_ids(ids_ref[...]))
    for got, out in ((ga_ref, ca_ref), (gb_ref, cb_ref)):
        remap(mine, lane_ids(got[FACE : FACE + 1, :]), got, match_ref, out)
    xa_out[...] = xa_ref[...] + cxa_ref[...]
    xb_out[...] = xb_ref[...] + cxb_ref[...]
    add_corners((xa_out, xb_out), sides("gx"), (ca_ref, cb_ref), sides("gy"))


def second_kernel(field_ref, ids_ref, xa_ref, xb_ref, ya_ref, yb_ref, out_ref, state_ref, halves_ref, edge_ref):
    state_ref[...] = field_ref[...]
    add_faces(state_ref, (xa_ref, xb_ref), (ya_ref, yb_ref), sides("gx"), sides("gy"))
    step(state_ref, ids_ref[...], out_ref, halves_ref, edge_ref)


def last_kernel(
    part_ref, ids_ref, xa_ref, xb_ref, ya_ref, yb_ref, hxa_ref, hxb_ref, hya_ref, hyb_ref, oya_ref, oyb_ref,
    out_ref, match_ref, cxa_ref, cxb_ref, cya_ref, cyb_ref,
):
    mine = lane_ids(flat_ids(ids_ref[...]))
    out_ref[...] = part_ref[...]
    for got, head, out, own in (
        (xa_ref, hxa_ref, cxa_ref, None),
        (xb_ref, hxb_ref, cxb_ref, None),
        (ya_ref, hya_ref, cya_ref, oya_ref),
        (yb_ref, hyb_ref, cyb_ref, oyb_ref),
    ):
        remap(mine, lane_ids(head[FACE : FACE + 1, :]), got, match_ref, out, own)
    add_faces(out_ref, (cxa_ref, cxb_ref), (cya_ref, cyb_ref), sides("gx"), sides("gy"))


def call(body, outs, scratch=(), flops=0, bytes_accessed=0):
    return pl.pallas_call(
        body,
        out_shape=[jax.ShapeDtypeStruct(shape, F32) for shape in outs],
        scratch_shapes=[pltpu.VMEM(shape, dtype) for shape, dtype in scratch],
        compiler_params=pltpu.CompilerParams(vmem_limit_bytes=40 * 2**20),
        cost_estimate=pl.CostEstimate(
            flops=flops, bytes_accessed=bytes_accessed, transcendentals=0
        ),
    )


def pairs(count, start):
    order = []
    for i in range(start, start + count, 2):
        a, b = i % count, (i + 1) % count
        order += [(a, b), (b, a)]
    return order


def exchange(value, axis, which):
    return lax.ppermute(value, axis, pairs(lax.axis_size(axis), which))


WHOLE = (SLOTS, ROWS, NZ)
SIDE = (FACE, NZ)
FIRST = (HEAD, NZ)
STEP_SCRATCH = [((SLOTS, ROWS, 2 * NZ), BF16), ((ROWS, 4 * NZ), BF16)]
MATCH = ((SLOTS, SLOTS, NZ), F32)


def shards(phase_fields, grain_ids):
    field = phase_fields.reshape(WHOLE)
    ids = grain_ids.reshape(NTZ, SLOTS)
    sya, syb, sxa, sxb = call(pack_kernel, [FIRST] * 4, bytes_accessed=3 << 20)(field, ids)
    gya, gyb = exchange(sya, "gy", 0), exchange(syb, "gy", 1)
    gxa, gxb = exchange(sxa, "gx", 0), exchange(sxb, "gx", 1)
    part, pya, pyb, pxa, pxb = call(
        first_kernel, [WHOLE] + [SIDE] * 4, STEP_SCRATCH, flops=4 << 30, bytes_accessed=4 << 20
    )(field, ids)
    pya, pyb, cxa, cxb = call(x_kernel, [SIDE] * 4, [MATCH], bytes_accessed=1 << 20)(
        ids, gxa, gxb, pya, pyb
    )
    gpya, gpyb = exchange(pya, "gy", 0), exchange(pyb, "gy", 1)
    pxa, pxb, cya, cyb = call(y_kernel, [SIDE] * 4, [MATCH], bytes_accessed=1 << 20)(
        ids, gya, gyb, pxa, pxb, cxa, cxb
    )
    gpxa, gpxb = exchange(pxa, "gx", 0), exchange(pxb, "gx", 1)
    (part,) = call(
        second_kernel, [WHOLE], [(WHOLE, F32)] + STEP_SCRATCH, flops=4 << 30, bytes_accessed=5 << 20
    )(part, ids, cxa, cxb, cya, cyb)
    (out,) = call(last_kernel, [WHOLE], [MATCH] + [(SIDE, F32)] * 4, bytes_accessed=5 << 20)(
        part, ids, gpxa, gpxb, gpya, gpyb, gxa, gxb, gya, gyb, sya, syb
    )
    return out.reshape(phase_fields.shape)


def solution(mesh):
    in_specs = (P(None, "gx", "gy", None), P("gx", "gy", None, None))
    out_specs = P(None, "gx", "gy", None)
    return jax.shard_map(shards, mesh=mesh, in_specs=in_specs, out_specs=out_specs, check_vma=False)
```

time: 491 us -> 45.3 us (0.09)
  the two profiles are of different devices: /device:TPU:0 before, /device:TPU:2 now
where the time goes in v1:
time: 45.3 us; the launch traced here: 45.2 us
  starting transfers between devices  21.9 us (48%)
  Pallas kernels  13.5 us (30%)
  waiting for transfers between devices  7.46 us (16%)
  local copies, waits for them, and re-layouts  2.28 us (5%)
    ppermute x8, starting transfers between devices, exchange(): return lax.ppermute(value, axis, pairs(lax.axis_size(axis), which))  21.9 us
    ppermute x8, waiting for transfers between devices, exchange(): return lax.ppermute(value, axis, pairs(lax.axis_size(axis), which))  7.46 us
    pallas_call x1, Pallas kernels, shards(): call(second_kernel, [WHOLE], [(WHOLE, F32)] + STEP_SCRATCH, flops=4 << 30...  4.41 us
    pallas_call x1, Pallas kernels, shards(): call(first_kernel, [WHOLE] + [SIDE] * 4, STEP_SCRATCH, flops=4 << 30, byt...  4.31 us
    pallas_call x1, Pallas kernels, shards(): call(last_kernel, [WHOLE], [MATCH] + [(SIDE, F32)] * 4, bytes_accessed=5...  2.96 us
    unnamed x6, local copies, waits for them, and re-layouts  2.28 us
  transfers between devices with their start and end apart: 8, of which 2 were waited for; matrix products, arithmetic and copies ran while one was open for 0% of the time, Pallas kernels for 23%

profile of v1, /device:TPU:2, one launch (start us, length us, event | category | flops | bytes accessed | tf_op | source)
XLA Modules:
  0.0 45.2 jit_solution(1282672805224772340)
XLA Ops:
  0.0 0.0 copy-start
  0.0 1.6 %copy-done = f32[16,16,16,128]{3,2,1,0:T(8,128)S(1)} copy-done((f32[16,16,16,128]{3,2,1,0:T(8,128)S(1)}, f32[16,16,16,128]{3,2,1,0:T(8,128)}, u32[]{:S(2)}) %copy-start) | copy-done | bytes 2097176
  1.6 0.0 copy-start.1
  1.6 0.7 %copy-done.1 = s32[1,1,8,16]{3,2,1,0:T(8,128)S(1)} copy-done((s32[1,1,8,16]{3,2,1,0:T(8,128)S(1)}, s32[1,1,8,16]{3,2,1,0:T(8,128)}, u32[]{:S(2)}) %copy-start.1) | copy-done | bytes 536
  2.3 0.2 shard_map.29
  2.5 0.1 collective-permute-start
  2.6 7.2 %collective-permute-start.1 = (f32[264,128]{1,0:T(8,128)S(1)}, f32[264,128]{1,0:T(8,128)S(1)}, u32[]{:S(2)}, u32[]{:S(2)}) collective-permute-start(f32[264,128]{1,0:T(8,128)S(1)} %get-tuple-element.24), channel_id=1, source_target_pairs={{8,16},{16,8},{24,32},{32,24},{40,48},{48,40},{56,64},{64,56},{72,... | collective-permute-start | bytes 405512 | tf_op jit(solution)/shard_map/ppermute | solution.py:213
  9.7 4.5 %collective-permute-start.2 = (f32[264,128]{1,0:T(8,128)S(1)}, f32[264,128]{1,0:T(8,128)S(1)}, u32[]{:S(2)}, u32[]{:S(2)}) collective-permute-start(f32[264,128]{1,0:T(8,128)S(1)} %get-tuple-element.29.oya_ref), channel_id=1, source_target_pairs={{0,1},{1,0},{2,3},{3,2},{4,5},{5,4},{6,7},{7,6},{8,9},{9,8},{10,11... | collective-permute-start | bytes 405512 | tf_op jit(solution)/shard_map/ppermute | solution.py:213
  14.2 0.0 copy-start.2
  14.2 1.4 %collective-permute-start.3 = (f32[264,128]{1,0:T(8,128)S(1)}, f32[264,128]{1,0:T(8,128)S(1)}, u32[]{:S(2)}, u32[]{:S(2)}) collective-permute-start(f32[264,128]{1,0:T(8,128)S(1)} %get-tuple-element.30.oyb_ref), channel_id=1, source_target_pairs={{1,2},{2,1},{3,4},{4,3},{5,6},{6,5},{7,0},{0,7},{9,10},{10,9},{11,... | collective-permute-start | bytes 405512 | tf_op jit(solution)/shard_map/ppermute | solution.py:213
  15.6 4.3 %shard_map.28 = (f32[16,256,128]{2,1,0:T(8,128)S(1)}, f32[256,128]{1,0:T(8,128)S(1)}, f32[256,128]{1,0:T(8,128)S(1)}, f32[256,128]{1,0:T(8,128)S(1)}, f32[256,128]{1,0:T(8,128)S(1)}) custom-call(f32[16,256,128]{2,1,0:T(8,128)S(1)} %bitcast.4, s32[8,16]{1,0:T(8,128)S(1)} %bitcast.6), custom_call_target="tpu_custom_call" | custom-call | flops 4294967296 | bytes 4194304 | tf_op jit(solution)/shard_map/pallas_call | solution.py:229
  19.9 0.0 collective-permute-done.ga_ref.hxa_ref
  20.0 0.0 collective-permute-done.1.gb_ref.hxb_ref
  20.0 0.8 %shard_map.30 = (f32[256,128]{1,0:T(8,128)S(1)}, f32[256,128]{1,0:T(8,128)S(1)}, f32[256,128]{1,0:T(8,128)S(1)}, f32[256,128]{1,0:T(8,128)S(1)}) custom-call(s32[8,16]{1,0:T(8,128)S(1)} %bitcast.7, f32[264,128]{1,0:T(8,128)S(1)} %collective-permute-done.ga_ref.hxa_ref, f32[264,128]{1,0:T(8,128)S(1)} %collective-permute-done.1.gb_ref.hxb_ref, ...), custom_call_target="tpu_custom_call" | custom-call | bytes 1048576 | tf_op jit(solution)/shard_map/pallas_call | solution.py:232
  20.8 5.6 %collective-permute-start.6 = (f32[256,128]{1,0:T(8,128)S(1)}, f32[256,128]{1,0:T(8,128)S(1)}, u32[]{:S(2)}, u32[]{:S(2)}) collective-permute-start(f32[256,128]{1,0:T(8,128)S(1)} %get-tuple-element.37), channel_id=1, source_target_pairs={{0,1},{1,0},{2,3},{3,2},{4,5},{5,4},{6,7},{7,6},{8,9},{9,8},{10,11... | collective-permute-start | bytes 393224 | tf_op jit(solution)/shard_map/ppermute | solution.py:213
  26.3 2.7 %collective-permute-start.7 = (f32[256,128]{1,0:T(8,128)S(1)}, f32[256,128]{1,0:T(8,128)S(1)}, u32[]{:S(2)}, u32[]{:S(2)}) collective-permute-start(f32[256,128]{1,0:T(8,128)S(1)} %get-tuple-element.38), channel_id=1, source_target_pairs={{1,2},{2,1},{3,4},{4,3},{5,6},{6,5},{7,0},{0,7},{9,10},{10,9},{11,... | collective-permute-start | bytes 393224 | tf_op jit(solution)/shard_map/ppermute | solution.py:213
  29.0 0.0 collective-permute-done.2.ga_ref.hya_ref
  29.0 0.0 collective-permute-done.3.gb_ref.hyb_ref
  29.0 0.8 %shard_map.31 = (f32[256,128]{1,0:T(8,128)S(1)}, f32[256,128]{1,0:T(8,128)S(1)}, f32[256,128]{1,0:T(8,128)S(1)}, f32[256,128]{1,0:T(8,128)S(1)}) custom-call(s32[8,16]{1,0:T(8,128)S(1)} %bitcast.8, f32[264,128]{1,0:T(8,128)S(1)} %collective-permute-done.2.ga_ref.hya_ref, f32[264,128]{1,0:T(8,128)S(1)} %collective-permute-done.3.gb_ref.hyb_ref, ...), custom_call_target="tpu_custom_call" | custom-call | bytes 1048576 | tf_op jit(solution)/shard_map/pallas_call | solution.py:236
  29.9 0.1 collective-permute-start.4
  30.0 0.4 collective-permute-start.5
  30.3 0.0 copy-done.2
  30.3 4.4 %shard_map.32.part_ref = f32[16,256,128]{2,1,0:T(8,128)S(1)} custom-call(f32[16,256,128]{2,1,0:T(8,128)S(1)} %get-tuple-element.22.field_ref, s32[8,16]{1,0:T(8,128)S(1)} %bitcast.9, f32[256,128]{1,0:T(8,128)S(1)} %get-tuple-element.27.cxa_ref.xa_ref, f32[256,128]{1,0:T(8,128)S(1)} %get-tuple-element.28.cxb_ref.xb_ref, ...), custom_call_target="tpu_custom_call" | custom-call | flops 4294967296 | bytes 5242880 | tf_op jit(solution)/shard_map/pallas_call | solution.py:240
  34.8 0.0 collective-permute-done.6.ya_ref
  34.8 5.9 %collective-permute-done.7.yb_ref = f32[256,128]{1,0:T(8,128)S(1)} collective-permute-done((f32[256,128]{1,0:T(8,128)S(1)}, f32[256,128]{1,0:T(8,128)S(1)}, u32[]{:S(2)}, u32[]{:S(2)}) %collective-permute-start.7) | collective-permute-done | bytes 131104 | tf_op jit(solution)/shard_map/ppermute | solution.py:213
  40.7 0.0 collective-permute-done.4.xa_ref
  40.7 1.5 %collective-permute-done.5.xb_ref = f32[256,128]{1,0:T(8,128)S(1)} collective-permute-done((f32[256,128]{1,0:T(8,128)S(1)}, f32[256,128]{1,0:T(8,128)S(1)}, u32[]{:S(2)}, u32[]{:S(2)}) %collective-permute-start.5) | collective-permute-done | bytes 131104 | tf_op jit(solution)/shard_map/ppermute | solution.py:213
  42.2 3.0 %shard_map.33 = f32[16,256,128]{2,1,0:T(8,128)} custom-call(f32[16,256,128]{2,1,0:T(8,128)S(1)} %shard_map.32.part_ref, s32[8,16]{1,0:T(8,128)S(1)} %bitcast.10, f32[256,128]{1,0:T(8,128)S(1)} %collective-permute-done.4.xa_ref, f32[256,128]{1,0:T(8,128)S(1)} %collective-permute-done.5.xb_ref, f32[256,128]{1,0:T(8,128)S(1)} %collective-permute-done.6.ya_ref, ...), custom_call_target="tpu_custom_call" | custom-call | bytes 5242880 | tf_op jit(solution)/shard_map/pallas_call | solution.py:243
Async XLA Ops:
  0.0 1.6 %copy-start = (f32[16,16,16,128]{3,2,1,0:T(8,128)S(1)}, f32[16,16,16,128]{3,2,1,0:T(8,128)}, u32[]{:S(2)}) copy-start(f32[16,16,16,128]{3,2,1,0:T(8,128)} %param.2) | copy-start | bytes 6291460
  1.6 0.7 %copy-start.1 = (s32[1,1,8,16]{3,2,1,0:T(8,128)S(1)}, s32[1,1,8,16]{3,2,1,0:T(8,128)}, u32[]{:S(2)}) copy-start(s32[1,1,8,16]{3,2,1,0:T(8,128)} %param.3) | copy-start | bytes 1540
  2.5 17.5 %collective-permute-start = (f32[264,128]{1,0:T(8,128)S(1)}, f32[264,128]{1,0:T(8,128)S(1)}, u32[]{:S(2)}, u32[]{:S(2)}) collective-permute-start(f32[264,128]{1,0:T(8,128)S(1)} %get-tuple-element.23), channel_id=1, source_target_pairs={{0,8},{8,0},{16,24},{24,16},{32,40},{40,32},{48,56},{56,48},{64,72... | collective-permute-start | bytes 405512 | tf_op jit(solution)/shard_map/ppermute | solution.py:213
  2.6 17.4 %collective-permute-start.1 = (f32[264,128]{1,0:T(8,128)S(1)}, f32[264,128]{1,0:T(8,128)S(1)}, u32[]{:S(2)}, u32[]{:S(2)}) collective-permute-start(f32[264,128]{1,0:T(8,128)S(1)} %get-tuple-element.24), channel_id=1, source_target_pairs={{8,16},{16,8},{24,32},{32,24},{40,48},{48,40},{56,64},{64,56},{72,... | collective-permute-start | bytes 405512 | tf_op jit(solution)/shard_map/ppermute | solution.py:213
  9.7 19.3 %collective-permute-start.2 = (f32[264,128]{1,0:T(8,128)S(1)}, f32[264,128]{1,0:T(8,128)S(1)}, u32[]{:S(2)}, u32[]{:S(2)}) collective-permute-start(f32[264,128]{1,0:T(8,128)S(1)} %get-tuple-element.29.oya_ref), channel_id=1, source_target_pairs={{0,1},{1,0},{2,3},{3,2},{4,5},{5,4},{6,7},{7,6},{8,9},{9,8},{10,11... | collective-permute-start | bytes 405512 | tf_op jit(solution)/shard_map/ppermute | solution.py:213
  14.2 16.1 %copy-start.2 = (s32[1,1,8,16]{3,2,1,0:T(8,128)S(1)}, s32[1,1,8,16]{3,2,1,0:T(8,128)}, u32[]{:S(2)}) copy-start(s32[1,1,8,16]{3,2,1,0:T(8,128)} %param.3) | copy-start | bytes 1540
  14.2 14.8 %collective-permute-start.3 = (f32[264,128]{1,0:T(8,128)S(1)}, f32[264,128]{1,0:T(8,128)S(1)}, u32[]{:S(2)}, u32[]{:S(2)}) collective-permute-start(f32[264,128]{1,0:T(8,128)S(1)} %get-tuple-element.30.oyb_ref), channel_id=1, source_target_pairs={{1,2},{2,1},{3,4},{4,3},{5,6},{6,5},{7,0},{0,7},{9,10},{10,9},{11,... | collective-permute-start | bytes 405512 | tf_op jit(solution)/shard_map/ppermute | solution.py:213
  20.8 14.0 %collective-permute-start.6 = (f32[256,128]{1,0:T(8,128)S(1)}, f32[256,128]{1,0:T(8,128)S(1)}, u32[]{:S(2)}, u32[]{:S(2)}) collective-permute-start(f32[256,128]{1,0:T(8,128)S(1)} %get-tuple-element.37), channel_id=1, source_target_pairs={{0,1},{1,0},{2,3},{3,2},{4,5},{5,4},{6,7},{7,6},{8,9},{9,8},{10,11... | collective-permute-start | bytes 393224 | tf_op jit(solution)/shard_map/ppermute | solution.py:213
  26.3 14.3 %collective-permute-start.7 = (f32[256,128]{1,0:T(8,128)S(1)}, f32[256,128]{1,0:T(8,128)S(1)}, u32[]{:S(2)}, u32[]{:S(2)}) collective-permute-start(f32[256,128]{1,0:T(8,128)S(1)} %get-tuple-element.38), channel_id=1, source_target_pairs={{1,2},{2,1},{3,4},{4,3},{5,6},{6,5},{7,0},{0,7},{9,10},{10,9},{11,... | collective-permute-start | bytes 393224 | tf_op jit(solution)/shard_map/ppermute | solution.py:213
  29.9 10.8 %collective-permute-start.4 = (f32[256,128]{1,0:T(8,128)S(1)}, f32[256,128]{1,0:T(8,128)S(1)}, u32[]{:S(2)}, u32[]{:S(2)}) collective-permute-start(f32[256,128]{1,0:T(8,128)S(1)} %get-tuple-element.35), channel_id=1, source_target_pairs={{0,8},{8,0},{16,24},{24,16},{32,40},{40,32},{48,56},{56,48},{64,72... | collective-permute-start | bytes 393224 | tf_op jit(solution)/shard_map/ppermute | solution.py:213
  30.0 12.2 %collective-permute-start.5 = (f32[256,128]{1,0:T(8,128)S(1)}, f32[256,128]{1,0:T(8,128)S(1)}, u32[]{:S(2)}, u32[]{:S(2)}) collective-permute-start(f32[256,128]{1,0:T(8,128)S(1)} %get-tuple-element.36), channel_id=1, source_target_pairs={{8,16},{16,8},{24,32},{32,24},{40,48},{48,40},{56,64},{64,56},{72,... | collective-permute-start | bytes 393224 | tf_op jit(solution)/shard_map/ppermute | solution.py:213

commit v2 on v1

v2 whole, which is shorter than its diff:
```python
import jax
import jax.numpy as jnp
from jax import lax
from jax.experimental import pallas as pl
from jax.experimental.pallas import tpu as pltpu
from jax.sharding import PartitionSpec as P

SLOTS = 16
TILE = 16
ROWS = TILE * TILE
NZ = 128
NTZ = NZ // TILE
FACE = SLOTS * TILE
SENT = SLOTS - 1
PART = SENT * TILE
HEAD = PART + 8
RATE = 0.025
HIGHEST = lax.Precision.HIGHEST
F32 = jnp.float32
BF16 = jnp.bfloat16


def iota(shape, dim):
    return lax.broadcasted_iota(jnp.int32, shape, dim)


def sides(axis):
    odd = lax.axis_index(axis) & 1
    return (TILE - 1) * (1 - odd), (TILE - 1) * odd


def flat_ids(ids):
    lane = iota((SLOTS, NZ), 1)
    spread = ((lane & 15) == iota((SLOTS, NZ), 0)).astype(F32)
    wide = jnp.dot(ids.astype(F32), spread, precision=HIGHEST, preferred_element_type=F32)
    own = (iota((NTZ, NZ), 1) >> 4) == iota((NTZ, NZ), 0)
    return jnp.sum(jnp.where(own, wide, 0.0), axis=0, keepdims=True)


def lane_ids(flat):
    pick = jnp.where((iota((SLOTS, NZ), 1) & 15) == iota((SLOTS, NZ), 0), flat, 0.0)
    group = ((iota((NZ, NZ), 0) >> 4) == (iota((NZ, NZ), 1) >> 4)).astype(F32)
    return jnp.dot(pick, group, precision=HIGHEST, preferred_element_type=F32)


def kept(mine):
    rows = []
    for s in range(SENT):
        row = jnp.where(mine[s : s + 1, :] >= 0.0, 1.0, 0.0)
        rows.append(row * rows[-1] if rows else row)
    return rows


def sent_ids(ids):
    rows = [
        jnp.where(row > 0.0, ids[s : s + 1, :], ids[s + 1 : s + 2, :])
        for s, row in enumerate(kept(ids))
    ]
    return jnp.concatenate(rows + [jnp.full((1, NZ), -2.0, F32)], axis=0)


def send(face_ref, mine, out_ref):
    for s, row in enumerate(kept(mine)):
        keep = jnp.broadcast_to(row, (TILE, NZ)) > 0.0
        here, after = (face_ref[t * TILE : (t + 1) * TILE, :] for t in (s, s + 1))
        out_ref[s * TILE : (s + 1) * TILE, :] = jnp.where(keep, here, after)


def matches(mine, other, match_ref):
    for s in range(SLOTS):
        row = mine[s : s + 1, :]
        match_ref[s] = jnp.where((other == row) & (row >= 0.0), RATE, 0.0)


def remap(plane, match_ref, out_ref, own_ref=None, count=SENT):
    for s in range(SLOTS):
        total = None
        if own_ref is not None:
            listed = RATE * jnp.sum(match_ref[s], axis=0, keepdims=True)
            total = listed * own_ref[s * TILE : (s + 1) * TILE, :]
        for t in range(count):
            term = match_ref[s, t : t + 1, :] * plane[t * TILE : (t + 1) * TILE, :]
            total = term if total is None else total + term
        out_ref[s * TILE : (s + 1) * TILE, :] = total


def take_x(field_ref, x):
    return field_ref[:, pl.ds(pl.multiple_of(x * TILE, TILE), TILE), :].reshape(FACE, NZ)


def take_y(field_ref, s, y):
    return field_ref[s, pl.ds(y, TILE, stride=TILE), :]


def add_faces(field_ref, x_faces, y_faces, xs, ys):
    for ref, x in zip(x_faces, xs):
        at = pl.ds(pl.multiple_of(x * TILE, TILE), TILE)
        field_ref[:, at, :] += ref[...].reshape(SLOTS, TILE, NZ)
    for ref, y in zip(y_faces, ys):
        for s in range(SLOTS):
            at = pl.ds(y, TILE, stride=TILE)
            field_ref[s, at, :] += ref[s * TILE : (s + 1) * TILE, :]


def step(field_ref, lists_ref, out_ref, halves_ref, edge_ref):
    flat = lists_ref[SLOTS : SLOTS + 1, :]
    for s in range(SLOTS):
        value = field_ref[s]
        high = value.astype(BF16)
        halves_ref[s, :, :NZ] = high
        halves_ref[s, :, NZ:] = (value - high.astype(F32)).astype(BF16)
    r, c = iota((2 * NZ, 2 * NZ), 0), iota((2 * NZ, 2 * NZ), 1)
    rz, cz = r & (NZ - 1), c & (NZ - 1)
    at = rz == (cz >> 4) * TILE + jnp.where(c < NZ, TILE - 1, 0)
    edges = jnp.zeros((ROWS, 2 * NZ), F32)
    for t in range(SLOTS):
        pick = jnp.where(at & ((c & 15) == t), 1.0, 0.0).astype(BF16)
        edges += jnp.dot(halves_ref[t], pick, preferred_element_type=F32)
    high = edges.astype(BF16)
    edge_ref[:, : 2 * NZ] = high
    edge_ref[:, 2 * NZ :] = (edges - high.astype(F32)).astype(BF16)
    eye = iota((NZ, NZ), 0) == iota((NZ, NZ), 1)
    column = jnp.sum(jnp.where(eye, flat, 0.0), axis=1, keepdims=True)
    column = jnp.concatenate([column, column], axis=0)
    row = jnp.concatenate([flat, flat], axis=1)
    hop = ((r >> 7) == (c >> 7)) & ((cz >> 4) == (((rz >> 4) + jnp.where(r < NZ, 1, 7)) & 7))
    match = jnp.where(hop & (column == row) & (column >= 0.0), 1.0, 0.0).astype(BF16)
    moved = jnp.dot(edge_ref[:, : 2 * NZ], match, preferred_element_type=F32)
    moved += jnp.dot(edge_ref[:, 2 * NZ :], match, preferred_element_type=F32)
    below, above = moved[:, :NZ], moved[:, NZ:]
    gap = jnp.abs(r - c)
    beside = (gap == TILE) | ((gap == 1) & ((r >> 4) == (c >> 4)))
    beside = jnp.where(beside, 1.0, 0.0).astype(BF16)
    r, c = iota((2 * NZ, NZ), 0) & (NZ - 1), iota((2 * NZ, NZ), 1)
    along = jnp.where((jnp.abs(r - c) == 1) & ((r >> 4) == (c >> 4)), 1.0, 0.0).astype(BF16)
    total = field_ref[0] * field_ref[0]
    for s in range(1, SLOTS):
        total += field_ref[s] * field_ref[s]
    base = 0.9 - 0.15 * total
    lane = iota((ROWS, NZ), 1) & 15
    for s in range(SLOTS):
        low = turn(below, -s)
        near = jnp.where(lane == 0, low, jnp.where(lane == TILE - 1, turn(above, TILE - 1 - s), 0.0))
        near += jnp.dot(halves_ref[s], along, preferred_element_type=F32)
        plane = jnp.dot(beside, halves_ref[s], preferred_element_type=F32)
        near += plane[:, :NZ] + plane[:, NZ:]
        value = field_ref[s]
        out_ref[s] = value * (base + 0.1 * (value * value)) + RATE * near


def turn(value, by, dim=1):
    by %= value.shape[dim]
    return pltpu.roll(value, by, dim) if by else value


def pack_kernel(
    field_ref, ids_ref, xa_ref, xb_ref, ya_ref, yb_ref, planes_ref, rows_ref, ids_vmem, face_ref, sems
):
    ids = pltpu.make_async_copy(ids_ref, ids_vmem, sems.at[4])
    planes = [
        pltpu.make_async_copy(field_ref.at[:, pl.ds(x, 1), :, :], planes_ref.at[i], sems.at[i])
        for i, x in enumerate((0, TILE - 1))
    ]
    rows = [
        pltpu.make_async_copy(field_ref.at[:, :, pl.ds(y, 1), :], rows_ref.at[i], sems.at[2 + i])
        for i, y in enumerate((0, TILE - 1))
    ]
    for copy in [ids] + planes + rows:
        copy.start()
    ids.wait()
    flat = flat_ids(ids_vmem[...])
    mine = lane_ids(flat)
    flat = jnp.broadcast_to(flat, (HEAD - PART, NZ))
    for copies, from_ref, refs, axis in (
        (planes, planes_ref, (xa_ref, xb_ref), "gx"),
        (rows, rows_ref, (ya_ref, yb_ref), "gy"),
    ):
        odd = lax.axis_index(axis) & 1
        for copy in copies:
            copy.wait()
        for n, ref in enumerate(refs):
            face_ref[...] = from_ref[(odd + 1 + n) % 2].reshape(FACE, NZ)
            send(face_ref, mine, ref)
            ref[PART:, :] = flat


def take_faces(field_ref, x_refs, y_refs):
    for ref, side in zip(x_refs, sides("gx")):
        ref[...] = take_x(field_ref, side)
    for ref, side in zip(y_refs, sides("gy")):
        for s in range(SLOTS):
            ref[s * TILE : (s + 1) * TILE, :] = take_y(field_ref, s, side)


def first_kernel(
    field_ref, ids_ref, out_ref, xa_ref, xb_ref, ya_ref, yb_ref, oya_ref, oyb_ref, lists_ref, halves_ref, edge_ref
):
    flat = flat_ids(ids_ref[...])
    lists_ref[:SLOTS, :] = lane_ids(flat)
    lists_ref[SLOTS:, :] = jnp.broadcast_to(flat, (8, NZ))
    step(field_ref, lists_ref, out_ref, halves_ref, edge_ref)
    take_faces(field_ref, (), (oya_ref, oyb_ref))
    take_faces(out_ref, (xa_ref, xb_ref), (ya_ref, yb_ref))


def arrive(lists_ref, gots, matchs, outs):
    for got, match, out in zip(gots, matchs, outs):
        matches(lists_ref[:SLOTS, :], sent_ids(lane_ids(got[PART : PART + 1, :])), match)
        remap(got, match, out)


def add_rows(out_ref, place, add_refs, add_places):
    for ref, there in zip(add_refs, add_places):
        out_ref[pl.ds(there, SLOTS, stride=TILE), :] += ref[pl.ds(place, SLOTS, stride=TILE), :]


def x_kernel(lists_ref, ga_ref, gb_ref, ya_ref, yb_ref, ya_out, yb_out, ca_ref, cb_ref, ma_ref, mb_ref, face_ref):
    arrive(lists_ref, (ga_ref, gb_ref), (ma_ref, mb_ref), (ca_ref, cb_ref))
    for out, part, y in zip((ya_out, yb_out), (ya_ref, yb_ref), sides("gy")):
        face_ref[...] = part[...]
        add_rows(face_ref, y, (ca_ref, cb_ref), sides("gx"))
        send(face_ref, lists_ref[:SLOTS, :], out)


def y_kernel(
    lists_ref, ga_ref, gb_ref, xa_ref, xb_ref, cxa_ref, cxb_ref,
    xa_out, xb_out, ca_ref, cb_ref, ma_ref, mb_ref, face_ref,
):
    arrive(lists_ref, (ga_ref, gb_ref), (ma_ref, mb_ref), (ca_ref, cb_ref))
    for out, part, add, x in zip((xa_out, xb_out), (xa_ref, xb_ref), (cxa_ref, cxb_ref), sides("gx")):
        face_ref[...] = part[...] + add[...]
        add_rows(face_ref, x, (ca_ref, cb_ref), sides("gy"))
        send(face_ref, lists_ref[:SLOTS, :], out)


def second_kernel(
    field_ref, lists_ref, cxa_ref, cxb_ref, cya_ref, cyb_ref,
    out_ref, xa_ref, xb_ref, ya_ref, yb_ref, state_ref, halves_ref, edge_ref,
):
    state_ref[...] = field_ref[...]
    add_faces(state_ref, (cxa_ref, cxb_ref), (cya_ref, cyb_ref), sides("gx"), sides("gy"))
    step(state_ref, lists_ref, out_ref, halves_ref, edge_ref)
    take_faces(out_ref, (xa_ref, xb_ref), (ya_ref, yb_ref))


def last_kernel(
    part_ref, gxa_ref, gxb_ref, gya_ref, gyb_ref, mxa_ref, mxb_ref, mya_ref, myb_ref, oya_ref, oyb_ref,
    fxa_ref, fxb_ref, fya_ref, fyb_ref, out_ref, cxa_ref, cxb_ref, face_ref, planes_ref, rows_ref, sems,
):
    del part_ref
    odd = lax.axis_index("gx") & 1
    for n, (got, match, face, out) in enumerate(
        ((gxa_ref, mxa_ref, fxa_ref, cxa_ref), (gxb_ref, mxb_ref, fxb_ref, cxb_ref))
    ):
        remap(got, match, out)
        planes_ref[(odd + 1 + n) % 2] = (out[...] + face[...]).reshape(SLOTS, 1, TILE, NZ)
    planes = [
        pltpu.make_async_copy(planes_ref.at[i], out_ref.at[:, pl.ds(x, 1), :, :], sems.at[i])
        for i, x in enumerate((0, TILE - 1))
    ]
    for copy in planes:
        copy.start()
    odd = lax.axis_index("gy") & 1
    for n, (got, match, own, face, y) in enumerate(zip(
        (gya_ref, gyb_ref), (mya_ref, myb_ref), (oya_ref, oyb_ref), (fya_ref, fyb_ref), sides("gy")
    )):
        remap(got, match, face_ref, own)
        add_rows(face_ref, y, (cxa_ref, cxb_ref), sides("gx"))
        rows_ref[(odd + 1 + n) % 2] = (face_ref[...] + face[...]).reshape(SLOTS, TILE, 1, NZ)
    for copy in planes:
        copy.wait()
    rows = [
        pltpu.make_async_copy(rows_ref.at[i], out_ref.at[:, :, pl.ds(y, 1), :], sems.at[2 + i])
        for i, y in enumerate((0, TILE - 1))
    ]
    for copy in rows:
        copy.start()
    for copy in rows:
        copy.wait()


def call(body, outs, scratch=(), flops=0, bytes_accessed=0, vmem=40, **specs):
    return pl.pallas_call(
        body,
        out_shape=[jax.ShapeDtypeStruct(shape, F32) for shape in outs],
        scratch_shapes=[pltpu.VMEM(*one) if isinstance(one, tuple) else one for one in scratch],
        compiler_params=pltpu.CompilerParams(vmem_limit_bytes=vmem * 2**20),
        cost_estimate=pl.CostEstimate(
            flops=flops, bytes_accessed=bytes_accessed, transcendentals=0
        ),
        **specs,
    )


def pairs(count, start):
    order = []
    for i in range(start, start + count, 2):
        a, b = i % count, (i + 1) % count
        order += [(a, b), (b, a)]
    return order


def exchange(value, axis, which):
    return lax.ppermute(value, axis, pairs(lax.axis_size(axis), which))


WHOLE = (SLOTS, ROWS, NZ)
SIDE = (FACE, NZ)
FIRST = (HEAD, NZ)
SECOND = (PART, NZ)
LISTS = (SLOTS + 8, NZ)
STEP_SCRATCH = [((SLOTS, ROWS, 2 * NZ), BF16), ((ROWS, 4 * NZ), BF16)]
MATCH = (SLOTS, SLOTS, NZ)
ANYWHERE = pl.BlockSpec(memory_space=pl.ANY)
HERE = pl.BlockSpec(memory_space=pltpu.VMEM)


def shards(phase_fields, grain_ids):
    field = phase_fields.reshape(WHOLE)
    ids = grain_ids.reshape(NTZ, SLOTS)
    sxa, sxb, sya, syb = call(
        pack_kernel,
        [FIRST] * 4,
        [
            ((2, SLOTS, 1, TILE, NZ), F32),
            ((2, SLOTS, TILE, 1, NZ), F32),
            ((NTZ, SLOTS), jnp.int32),
            (SIDE, F32),
            pltpu.SemaphoreType.DMA((5,)),
        ],
        bytes_accessed=3 << 20,
        vmem=62,
        in_specs=[ANYWHERE, ANYWHERE],
    )(phase_fields, ids)
    gxa, gxb = exchange(sxa, "gx", 0), exchange(sxb, "gx", 1)
    gya, gyb = exchange(sya, "gy", 0), exchange(syb, "gy", 1)
    part, pxa, pxb, pya, pyb, oya, oyb, lists = call(
        first_kernel,
        [WHOLE] + [SIDE] * 6 + [LISTS],
        STEP_SCRATCH,
        flops=4 << 30,
        bytes_accessed=4 << 20,
    )(field, ids)
    tya, tyb, cxa, cxb, mxa, mxb = call(
        x_kernel, [SECOND] * 2 + [SIDE] * 2 + [MATCH] * 2, [(SIDE, F32)], bytes_accessed=1 << 20
    )(lists, gxa, gxb, pya, pyb)
    gpya, gpyb = exchange(tya, "gy", 0), exchange(tyb, "gy", 1)
    txa, txb, cya, cyb, mya, myb = call(
        y_kernel, [SECOND] * 2 + [SIDE] * 2 + [MATCH] * 2, [(SIDE, F32)], bytes_accessed=1 << 20
    )(lists, gya, gyb, pxa, pxb, cxa, cxb)
    gpxa, gpxb = exchange(txa, "gx", 0), exchange(txb, "gx", 1)
    part, fxa, fxb, fya, fyb = call(
        second_kernel,
        [WHOLE] + [SIDE] * 4,
        [(WHOLE, F32)] + STEP_SCRATCH,
        flops=4 << 30,
        bytes_accessed=5 << 20,
    )(part, lists, cxa, cxb, cya, cyb)
    (out,) = call(
        last_kernel,
        [phase_fields.shape],
        [
            (SIDE, F32),
            (SIDE, F32),
            (SIDE, F32),
            ((2, SLOTS, 1, TILE, NZ), F32),
            ((2, SLOTS, TILE, 1, NZ), F32),
            pltpu.SemaphoreType.DMA((4,)),
        ],
        bytes_accessed=5 << 20,
        in_specs=[ANYWHERE] + [HERE] * 14,
        out_specs=[ANYWHERE],
        input_output_aliases={0: 0},
    )(
        part.reshape(phase_fields.shape), gpxa, gpxb, gpya, gpyb, mxa, mxb, mya, myb, oya, oyb, fxa, fxb, fya, fyb
    )
    return out


def solution(mesh):
    in_specs = (P(None, "gx", "gy", None), P("gx", "gy", None, None))
    out_specs = P(None, "gx", "gy", None)
    return jax.shard_map(shards, mesh=mesh, in_specs=in_specs, out_specs=out_specs, check_vma=False)
```

time: 45.3 us -> 43.2 us (0.954)
  waiting for transfers between devices: 7.46 us -> 6.25 us
  local copies, waits for them, and re-layouts: 2.28 us -> 1.59 us
    ppermute x8, waiting for transfers between devices: 7.46 us -> 6.25 us  [exchange(): return lax.ppermute(value, axis, pairs(lax.axis_size(axis), which))]
    unnamed x6 -> x4, local copies, waits for them, and re-layouts: 2.28 us -> 1.59 us
  transfers between devices with their start and end apart: 8 -> 8, of which waited for: 2 -> 2; matrix products, arithmetic and copies ran while one was open for 0% -> 0% of each run, Pallas kernels for 23% -> 22%
where the time goes in v2:
time: 43.2 us; the launch traced here: 43 us
  starting transfers between devices  21.8 us (50%)
  Pallas kernels  13.2 us (31%)
  waiting for transfers between devices  6.25 us (14%)
  local copies, waits for them, and re-layouts  1.59 us (4%)
    ppermute x8, starting transfers between devices, exchange(): return lax.ppermute(value, axis, pairs(lax.axis_size(axis), which))  21.8 us
    ppermute x8, waiting for transfers between devices, exchange(): return lax.ppermute(value, axis, pairs(lax.axis_size(axis), which))  6.25 us
    pallas_call x1, Pallas kernels, shards(): call(second_kernel, [WHOLE] + [SIDE] * 4, [(WHOLE, F32)] + STEP_SCRATCH,...  4.67 us
    pallas_call x1, Pallas kernels, shards(): call(first_kernel, [WHOLE] + [SIDE] * 6 + [LISTS], STEP_SCRATCH, flops=4...  3.52 us
    pallas_call x1, Pallas kernels, shards(): call(pack_kernel, [FIRST] * 4, [((2, SLOTS, 1, TILE, NZ), F32), ((2, SLOT...  2.02 us
    pallas_call x1, Pallas kernels, shards(): call(last_kernel, [phase_fields.shape], [(SIDE, F32), (SIDE, F32), (SIDE,...  1.71 us
    unnamed x4, local copies, waits for them, and re-layouts  1.59 us
  transfers between devices with their start and end apart: 8, of which 2 were waited for; matrix products, arithmetic and copies ran while one was open for 0% of the time, Pallas kernels for 22%

profile of v2, /device:TPU:2, one launch (start us, length us, event | category | flops | bytes accessed | tf_op | source)
XLA Modules:
  0.0 43.0 jit_solution(3828204783545999452)
XLA Ops:
  0.0 0.0 copy-start.1
  0.0 2.0 %shard_map.29 = (f32[248,128]{1,0:T(8,128)}, f32[248,128]{1,0:T(8,128)}, f32[248,128]{1,0:T(8,128)}, f32[248,128]{1,0:T(8,128)}) custom-call(f32[16,16,16,128]{3,2,1,0:T(8,128)} %field_ref.1, s32[8,16]{1,0:T(8,128)} %bitcast.4), custom_call_target="tpu_custom_call" | custom-call | bytes 3145728 | tf_op jit(solution)/shard_map/pallas_call | solution.py:321
  2.0 0.1 collective-permute-start
  2.1 7.2 %collective-permute-start.1 = (f32[248,128]{1,0:T(8,128)}, f32[248,128]{1,0:T(8,128)S(1)}, u32[]{:S(2)}, u32[]{:S(2)}) collective-permute-start(f32[248,128]{1,0:T(8,128)} %get-tuple-element.37), channel_id=1, source_target_pairs={{8,16},{16,8},{24,32},{32,24},{40,48},{48,40},{56,64},{64,56},{72,... | collective-permute-start | bytes 380936 | tf_op jit(solution)/shard_map/ppermute | solution.py:304
  9.3 4.5 %collective-permute-start.2 = (f32[248,128]{1,0:T(8,128)}, f32[248,128]{1,0:T(8,128)S(1)}, u32[]{:S(2)}, u32[]{:S(2)}) collective-permute-start(f32[248,128]{1,0:T(8,128)} %get-tuple-element.42), channel_id=1, source_target_pairs={{0,1},{1,0},{2,3},{3,2},{4,5},{5,4},{6,7},{7,6},{8,9},{9,8},{10,11... | collective-permute-start | bytes 380936 | tf_op jit(solution)/shard_map/ppermute | solution.py:304
  13.8 1.4 %collective-permute-start.3 = (f32[248,128]{1,0:T(8,128)}, f32[248,128]{1,0:T(8,128)S(1)}, u32[]{:S(2)}, u32[]{:S(2)}) collective-permute-start(f32[248,128]{1,0:T(8,128)} %get-tuple-element.43), channel_id=1, source_target_pairs={{1,2},{2,1},{3,4},{4,3},{5,6},{6,5},{7,0},{0,7},{9,10},{10,9},{11,... | collective-permute-start | bytes 380936 | tf_op jit(solution)/shard_map/ppermute | solution.py:304
  15.2 0.0 copy-done.1
  15.2 0.0 copy-start
  15.2 1.6 %copy-done = f32[16,16,16,128]{3,2,1,0:T(8,128)S(1)} copy-done((f32[16,16,16,128]{3,2,1,0:T(8,128)S(1)}, f32[16,16,16,128]{3,2,1,0:T(8,128)}, u32[]{:S(2)}) %copy-start) | copy-done | bytes 2097176
  16.8 3.5 %shard_map.28 = (f32[16,256,128]{2,1,0:T(8,128)S(1)}, f32[256,128]{1,0:T(8,128)S(1)}, f32[256,128]{1,0:T(8,128)S(1)}, f32[256,128]{1,0:T(8,128)S(1)}, f32[256,12...) custom-call(f32[16,256,128]{2,1,0:T(8,128)S(1)} %bitcast.3, ...), custom_call_target="tpu_custom_call" | custom-call | flops 4294967296 | bytes 4194304 | tf_op jit(solution)/shard_map/pallas_call | solution.py:337
  20.3 0.0 collective-permute-done.ga_ref
  20.3 0.0 collective-permute-done.1.gb_ref
  20.4 0.6 %shard_map.30 = (f32[240,128]{1,0:T(8,128)S(1)}, f32[240,128]{1,0:T(8,128)S(1)}, f32[256,128]{1,0:T(8,128)S(1)}, f32[256,128]{1,0:T(8,128)S(1)}, f32[16,16,128]{2,1,0:T(8,128)S(1)}, /*index=5*/f32[16,16,128]{2,1,0:T(8,128)S(1)}) custom-call(f32[24,128]{1,0:T(8,128)S(1)} %get-tuple-element.35.lists_ref, f32[248,128]{1,0:T(8,128)S(1)} %collective-permute-done.ga_ref, ...), custom_call_target="tpu_custom_call" | custom-call | bytes 1048576 | tf_op jit(solution)/shard_map/pallas_call | solution.py:344
  21.0 5.5 %collective-permute-start.6 = (f32[240,128]{1,0:T(8,128)S(1)}, f32[240,128]{1,0:T(8,128)S(1)}, u32[]{:S(2)}, u32[]{:S(2)}) collective-permute-start(f32[240,128]{1,0:T(8,128)S(1)} %get-tuple-element.51), channel_id=1, source_target_pairs={{0,1},{1,0},{2,3},{3,2},{4,5},{5,4},{6,7},{7,6},{8,9},{9,8},{10,11... | collective-permute-start | bytes 368648 | tf_op jit(solution)/shard_map/ppermute | solution.py:304
  26.5 2.7 %collective-permute-start.7 = (f32[240,128]{1,0:T(8,128)S(1)}, f32[240,128]{1,0:T(8,128)S(1)}, u32[]{:S(2)}, u32[]{:S(2)}) collective-permute-start(f32[240,128]{1,0:T(8,128)S(1)} %get-tuple-element.52), channel_id=1, source_target_pairs={{1,2},{2,1},{3,4},{4,3},{5,6},{6,5},{7,0},{0,7},{9,10},{10,9},{11,... | collective-permute-start | bytes 368648 | tf_op jit(solution)/shard_map/ppermute | solution.py:304
  29.2 0.0 collective-permute-done.2.ga_ref
  29.2 0.0 collective-permute-done.3.gb_ref
  29.2 0.6 %shard_map.31 = (f32[240,128]{1,0:T(8,128)S(1)}, f32[240,128]{1,0:T(8,128)S(1)}, f32[256,128]{1,0:T(8,128)S(1)}, f32[256,128]{1,0:T(8,128)S(1)}, f32[16,16,128]{2,1,0:T(8,128)S(1)}, /*index=5*/f32[16,16,128]{2,1,0:T(8,128)S(1)}) custom-call(f32[24,128]{1,0:T(8,128)S(1)} %get-tuple-element.35.lists_ref, f32[248,128]{1,0:T(8,128)S(1)} %collective-permute-done.2.ga_ref, ...), custom_call_target="tpu_custom_call" | custom-call | bytes 1048576 | tf_op jit(solution)/shard_map/pallas_call | solution.py:348
  29.9 0.1 collective-permute-start.4
  30.0 0.3 collective-permute-start.5
  30.3 4.7 %shard_map.32 = (f32[16,256,128]{2,1,0:T(8,128)}, f32[256,128]{1,0:T(8,128)S(1)}, f32[256,128]{1,0:T(8,128)S(1)}, f32[256,128]{1,0:T(8,128)S(1)}, f32[256,128]{1,0:T(8,128)S(1)}) custom-call(f32[16,256,128]{2,1,0:T(8,128)S(1)} %get-tuple-element.34.field_ref, f32[24,128]{1,0:T(8,128)S(1)} %get-tuple-element.35.lists_ref, ...), custom_call_target="tpu_custom_call" | custom-call | flops 4294967296 | bytes 5242880 | tf_op jit(solution)/shard_map/pallas_call | solution.py:352
  34.9 0.0 collective-permute-done.6.gya_ref
  34.9 5.3 %collective-permute-done.7.gyb_ref = f32[240,128]{1,0:T(8,128)S(1)} collective-permute-done((f32[240,128]{1,0:T(8,128)S(1)}, f32[240,128]{1,0:T(8,128)S(1)}, u32[]{:S(2)}, u32[]{:S(2)}) %collective-permute-start.7) | collective-permute-done | bytes 122912 | tf_op jit(solution)/shard_map/ppermute | solution.py:304
  40.2 0.0 collective-permute-done.4.gxa_ref
  40.2 1.0 %collective-permute-done.5.gxb_ref = f32[240,128]{1,0:T(8,128)S(1)} collective-permute-done((f32[240,128]{1,0:T(8,128)S(1)}, f32[240,128]{1,0:T(8,128)S(1)}, u32[]{:S(2)}, u32[]{:S(2)}) %collective-permute-start.5) | collective-permute-done | bytes 122912 | tf_op jit(solution)/shard_map/ppermute | solution.py:304
  41.2 1.7 %shard_map.33 = f32[16,16,16,128]{3,2,1,0:T(8,128)} custom-call(f32[16,16,16,128]{3,2,1,0:T(8,128)} %bitcast.6, f32[240,128]{1,0:T(8,128)S(1)} %collective-permute-done.4.gxa_ref, f32[240,128]{1,0:T(8,128)S(1)} %collective-permute-done.5.gxb_ref, f32[240,128]{1,0:T(8,128)S(1)} %collective-permute-done.6.gya_ref, ...), custom_call_target="tpu_custom_call", output_to_operand_aliasing={{}: (0, {})} | custom-call | bytes 5242880 | tf_op jit(solution)/shard_map/pallas_call | solution.py:359
Async XLA Ops:
  0.0 15.2 %copy-start.1 = (s32[1,1,8,16]{3,2,1,0:T(8,128)S(1)}, s32[1,1,8,16]{3,2,1,0:T(8,128)}, u32[]{:S(2)}) copy-start(s32[1,1,8,16]{3,2,1,0:T(8,128)} %param.3) | copy-start | bytes 1540
  2.0 18.3 %collective-permute-start = (f32[248,128]{1,0:T(8,128)}, f32[248,128]{1,0:T(8,128)S(1)}, u32[]{:S(2)}, u32[]{:S(2)}) collective-permute-start(f32[248,128]{1,0:T(8,128)} %get-tuple-element.36), channel_id=1, source_target_pairs={{0,8},{8,0},{16,24},{24,16},{32,40},{40,32},{48,56},{56,48},{64,72... | collective-permute-start | bytes 380936 | tf_op jit(solution)/shard_map/ppermute | solution.py:304
  2.1 18.2 %collective-permute-start.1 = (f32[248,128]{1,0:T(8,128)}, f32[248,128]{1,0:T(8,128)S(1)}, u32[]{:S(2)}, u32[]{:S(2)}) collective-permute-start(f32[248,128]{1,0:T(8,128)} %get-tuple-element.37), channel_id=1, source_target_pairs={{8,16},{16,8},{24,32},{32,24},{40,48},{48,40},{56,64},{64,56},{72,... | collective-permute-start | bytes 380936 | tf_op jit(solution)/shard_map/ppermute | solution.py:304
  9.3 19.9 %collective-permute-start.2 = (f32[248,128]{1,0:T(8,128)}, f32[248,128]{1,0:T(8,128)S(1)}, u32[]{:S(2)}, u32[]{:S(2)}) collective-permute-start(f32[248,128]{1,0:T(8,128)} %get-tuple-element.42), channel_id=1, source_target_pairs={{0,1},{1,0},{2,3},{3,2},{4,5},{5,4},{6,7},{7,6},{8,9},{9,8},{10,11... | collective-permute-start | bytes 380936 | tf_op jit(solution)/shard_map/ppermute | solution.py:304
  13.8 15.4 %collective-permute-start.3 = (f32[248,128]{1,0:T(8,128)}, f32[248,128]{1,0:T(8,128)S(1)}, u32[]{:S(2)}, u32[]{:S(2)}) collective-permute-start(f32[248,128]{1,0:T(8,128)} %get-tuple-element.43), channel_id=1, source_target_pairs={{1,2},{2,1},{3,4},{4,3},{5,6},{6,5},{7,0},{0,7},{9,10},{10,9},{11,... | collective-permute-start | bytes 380936 | tf_op jit(solution)/shard_map/ppermute | solution.py:304
  15.2 1.6 %copy-start = (f32[16,16,16,128]{3,2,1,0:T(8,128)S(1)}, f32[16,16,16,128]{3,2,1,0:T(8,128)}, u32[]{:S(2)}) copy-start(f32[16,16,16,128]{3,2,1,0:T(8,128)} %field_ref.1) | copy-start | bytes 6291460
  21.0 13.9 %collective-permute-start.6 = (f32[240,128]{1,0:T(8,128)S(1)}, f32[240,128]{1,0:T(8,128)S(1)}, u32[]{:S(2)}, u32[]{:S(2)}) collective-permute-start(f32[240,128]{1,0:T(8,128)S(1)} %get-tuple-element.51), channel_id=1, source_target_pairs={{0,1},{1,0},{2,3},{3,2},{4,5},{5,4},{6,7},{7,6},{8,9},{9,8},{10,11... | collective-permute-start | bytes 368648 | tf_op jit(solution)/shard_map/ppermute | solution.py:304
  26.5 13.7 %collective-permute-start.7 = (f32[240,128]{1,0:T(8,128)S(1)}, f32[240,128]{1,0:T(8,128)S(1)}, u32[]{:S(2)}, u32[]{:S(2)}) collective-permute-start(f32[240,128]{1,0:T(8,128)S(1)} %get-tuple-element.52), channel_id=1, source_target_pairs={{1,2},{2,1},{3,4},{4,3},{5,6},{6,5},{7,0},{0,7},{9,10},{10,9},{11,... | collective-permute-start | bytes 368648 | tf_op jit(solution)/shard_map/ppermute | solution.py:304
  29.9 10.3 %collective-permute-start.4 = (f32[240,128]{1,0:T(8,128)S(1)}, f32[240,128]{1,0:T(8,128)S(1)}, u32[]{:S(2)}, u32[]{:S(2)}) collective-permute-start(f32[240,128]{1,0:T(8,128)S(1)} %get-tuple-element.49), channel_id=1, source_target_pairs={{0,8},{8,0},{16,24},{24,16},{32,40},{40,32},{48,56},{56,48},{64,72... | collective-permute-start | bytes 368648 | tf_op jit(solution)/shard_map/ppermute | solution.py:304
  30.0 11.2 %collective-permute-start.5 = (f32[240,128]{1,0:T(8,128)S(1)}, f32[240,128]{1,0:T(8,128)S(1)}, u32[]{:S(2)}, u32[]{:S(2)}) collective-permute-start(f32[240,128]{1,0:T(8,128)S(1)} %get-tuple-element.50), channel_id=1, source_target_pairs={{8,16},{16,8},{24,32},{32,24},{40,48},{48,40},{56,64},{64,56},{72,... | collective-permute-start | bytes 368648 | tf_op jit(solution)/shard_map/ppermute | solution.py:304

commit v3 on v2

--- a/solution.py
+++ b/solution.py
@@ -243,39 +243,47 @@
     take_faces(out_ref, (xa_ref, xb_ref), (ya_ref, yb_ref))
 
 
-def last_kernel(
-    part_ref, gxa_ref, gxb_ref, gya_ref, gyb_ref, mxa_ref, mxb_ref, mya_ref, myb_ref, oya_ref, oyb_ref,
-    fxa_ref, fxb_ref, fya_ref, fyb_ref, out_ref, cxa_ref, cxb_ref, face_ref, planes_ref, rows_ref, sems,
+def last_y_kernel(
+    part_ref, gya_ref, gyb_ref, mya_ref, myb_ref, oya_ref, oyb_ref, fya_ref, fyb_ref,
+    out_ref, cya_ref, cyb_ref, rows_ref, sems,
+):
+    del part_ref
+    odd = lax.axis_index("gy") & 1
+    for n, (got, match, own, face, out) in enumerate((
+        (gya_ref, mya_ref, oya_ref, fya_ref, cya_ref),
+        (gyb_ref, myb_ref, oyb_ref, fyb_ref, cyb_ref),
+    )):
+        remap(got, match, out, own)
+        rows_ref[(odd + 1 + n) % 2] = (out[...] + face[...]).reshape(SLOTS, TILE, 1, NZ)
+    copies = [
+        pltpu.make_async_copy(rows_ref.at[i], out_ref.at[:, :, pl.ds(y, 1), :], sems.at[i])
+        for i, y in enumerate((0, TILE - 1))
+    ]
+    for copy in copies:
+        copy.start()
+    for copy in copies:
+        copy.wait()
+
+
+def last_x_kernel(
+    part_ref, gxa_ref, gxb_ref, mxa_ref, mxb_ref, fxa_ref, fxb_ref, cya_ref, cyb_ref,
+    out_ref, face_ref, planes_ref, sems,
 ):
     del part_ref
     odd = lax.axis_index("gx") & 1
-    for n, (got, match, face, out) in enumerate(
-        ((gxa_ref, mxa_ref, fxa_ref, cxa_ref), (gxb_ref, mxb_ref, fxb_ref, cxb_ref))
+    for n, (got, match, face, x) in enumerate(
+        zip((gxa_ref, gxb_ref), (mxa_ref, mxb_ref), (fxa_ref, fxb_ref), sides("gx"))
     ):
-        remap(got, match, out)
-        planes_ref[(odd + 1 + n) % 2] = (out[...] + face[...]).reshape(SLOTS, 1, TILE, NZ)
-    planes = [
+        remap(got, match, face_ref)
+        add_rows(face_ref, x, (cya_ref, cyb_ref), sides("gy"))
+        planes_ref[(odd + 1 + n) % 2] = (face_ref[...] + face[...]).reshape(SLOTS, 1, TILE, NZ)
+    copies = [
         pltpu.make_async_copy(planes_ref.at[i], out_ref.at[:, pl.ds(x, 1), :, :], sems.at[i])
         for i, x in enumerate((0, TILE - 1))
     ]
-    for copy in planes:
+    for copy in copies:
         copy.start()
-    odd = lax.axis_index("gy") & 1
-    for n, (got, match, own, face, y) in enumerate(zip(
-        (gya_ref, gyb_ref), (mya_ref, myb_ref), (oya_ref, oyb_ref), (fya_ref, fyb_ref), sides("gy")
-    )):
-        remap(got, match, face_ref, own)
-        add_rows(face_ref, y, (cxa_ref, cxb_ref), sides("gx"))
-        rows_ref[(odd + 1 + n) % 2] = (face_ref[...] + face[...]).reshape(SLOTS, TILE, 1, NZ)
-    for copy in planes:
-        copy.wait()
-    rows = [
-        pltpu.make_async_copy(rows_ref.at[i], out_ref.at[:, :, pl.ds(y, 1), :], sems.at[2 + i])
-        for i, y in enumerate((0, TILE - 1))
-    ]
-    for copy in rows:
-        copy.start()
-    for copy in rows:
+    for copy in copies:
         copy.wait()
 
 
@@ -356,24 +364,24 @@
         flops=4 << 30,
         bytes_accessed=5 << 20,
     )(part, lists, cxa, cxb, cya, cyb)
+    part, cya, cyb = call(
+        last_y_kernel,
+        [phase_fields.shape] + [SIDE] * 2,
+        [((2, SLOTS, TILE, 1, NZ), F32), pltpu.SemaphoreType.DMA((2,))],
+        bytes_accessed=1 << 20,
+        in_specs=[ANYWHERE] + [HERE] * 8,
+        out_specs=[ANYWHERE, HERE, HERE],
+        input_output_aliases={0: 0},
+    )(part.reshape(phase_fields.shape), gpya, gpyb, mya, myb, oya, oyb, fya, fyb)
     (out,) = call(
-        last_kernel,
+        last_x_kernel,
         [phase_fields.shape],
-        [
-            (SIDE, F32),
-            (SIDE, F32),
-            (SIDE, F32),
-            ((2, SLOTS, 1, TILE, NZ), F32),
-            ((2, SLOTS, TILE, 1, NZ), F32),
-            pltpu.SemaphoreType.DMA((4,)),
-        ],
-        bytes_accessed=5 << 20,
-        in_specs=[ANYWHERE] + [HERE] * 14,
+        [(SIDE, F32), ((2, SLOTS, 1, TILE, NZ), F32), pltpu.SemaphoreType.DMA((2,))],
+        bytes_accessed=1 << 20,
+        in_specs=[ANYWHERE] + [HERE] * 8,
         out_specs=[ANYWHERE],
         input_output_aliases={0: 0},
-    )(
-        part.reshape(phase_fields.shape), gpxa, gpxb, gpya, gpyb, mxa, mxb, mya, myb, oya, oyb, fxa, fxb, fya, fyb
-    )
+    )(part, gpxa, gpxb, mxa, mxb, fxa, fxb, cya, cyb)
     return out
 
 

time: 43.2 us -> 42.8 us (level)
  waiting for transfers between devices: 6.25 us -> 5.28 us
  Pallas kernels: 13.2 us -> 13.8 us
    ppermute x8, waiting for transfers between devices: 6.25 us -> 5.28 us  [exchange(): return lax.ppermute(value, axis, pairs(lax.axis_size(axis), which))]
    pallas_call x1 -> x2, Pallas kernels: 1.71 us -> 2.33 us  [the longest x1 1.28 us: shards(): call(last_y_kernel, [phase_fields.shape] + [SIDE] * 2, [((2, SLOTS, TILE,...]
  transfers between devices with their start and end apart: 8 -> 8, of which waited for: 2 -> 1; matrix products, arithmetic and copies ran while one was open for 0% -> 0% of each run, Pallas kernels for 22% -> 25%
where the time goes in v3:
time: 42.8 us; the launch traced here: 42.7 us
  starting transfers between devices  21.8 us (51%)
  Pallas kernels  13.8 us (32%)
  waiting for transfers between devices  5.28 us (12%)
  local copies, waits for them, and re-layouts  1.59 us (4%)
    ppermute x8, starting transfers between devices, exchange(): return lax.ppermute(value, axis, pairs(lax.axis_size(axis), which))  21.8 us
    ppermute x8, waiting for transfers between devices, exchange(): return lax.ppermute(value, axis, pairs(lax.axis_size(axis), which))  5.28 us
    pallas_call x1, Pallas kernels, shards(): call(second_kernel, [WHOLE] + [SIDE] * 4, [(WHOLE, F32)] + STEP_SCRATCH,...  4.67 us
    pallas_call x1, Pallas kernels, shards(): call(first_kernel, [WHOLE] + [SIDE] * 6 + [LISTS], STEP_SCRATCH, flops=4...  3.52 us
    pallas_call x1, Pallas kernels, shards(): call(pack_kernel, [FIRST] * 4, [((2, SLOTS, 1, TILE, NZ), F32), ((2, SLOT...  2.02 us
    unnamed x4, local copies, waits for them, and re-layouts  1.59 us
    pallas_call x1, Pallas kernels, shards(): call(last_y_kernel, [phase_fields.shape] + [SIDE] * 2, [((2, SLOTS, TILE,...  1.28 us
    pallas_call x1, Pallas kernels, shards(): call(last_x_kernel, [phase_fields.shape], [(SIDE, F32), ((2, SLOTS, 1, TI...  1.05 us
  transfers between devices with their start and end apart: 8, of which 1 were waited for; matrix products, arithmetic and copies ran while one was open for 0% of the time, Pallas kernels for 25%

profile of v3, /device:TPU:2, one launch (start us, length us, event | category | flops | bytes accessed | tf_op | source)
XLA Modules:
  0.0 42.7 jit_solution(5408821764179965374)
XLA Ops:
  0.0 0.0 copy-start.1
  0.0 2.0 %shard_map.29 = (f32[248,128]{1,0:T(8,128)}, f32[248,128]{1,0:T(8,128)}, f32[248,128]{1,0:T(8,128)}, f32[248,128]{1,0:T(8,128)}) custom-call(f32[16,16,16,128]{3,2,1,0:T(8,128)} %field_ref.1, s32[8,16]{1,0:T(8,128)} %bitcast.4), custom_call_target="tpu_custom_call" | custom-call | bytes 3145728 | tf_op jit(solution)/shard_map/pallas_call | solution.py:329
  2.0 0.1 collective-permute-start
  2.1 7.2 %collective-permute-start.1 = (f32[248,128]{1,0:T(8,128)}, f32[248,128]{1,0:T(8,128)S(1)}, u32[]{:S(2)}, u32[]{:S(2)}) collective-permute-start(f32[248,128]{1,0:T(8,128)} %get-tuple-element.40), channel_id=1, source_target_pairs={{8,16},{16,8},{24,32},{32,24},{40,48},{48,40},{56,64},{64,56},{72,... | collective-permute-start | bytes 380936 | tf_op jit(solution)/shard_map/ppermute | solution.py:312
  9.3 4.5 %collective-permute-start.2 = (f32[248,128]{1,0:T(8,128)}, f32[248,128]{1,0:T(8,128)S(1)}, u32[]{:S(2)}, u32[]{:S(2)}) collective-permute-start(f32[248,128]{1,0:T(8,128)} %get-tuple-element.45), channel_id=1, source_target_pairs={{0,1},{1,0},{2,3},{3,2},{4,5},{5,4},{6,7},{7,6},{8,9},{9,8},{10,11... | collective-permute-start | bytes 380936 | tf_op jit(solution)/shard_map/ppermute | solution.py:312
  13.8 1.4 %collective-permute-start.3 = (f32[248,128]{1,0:T(8,128)}, f32[248,128]{1,0:T(8,128)S(1)}, u32[]{:S(2)}, u32[]{:S(2)}) collective-permute-start(f32[248,128]{1,0:T(8,128)} %get-tuple-element.46), channel_id=1, source_target_pairs={{1,2},{2,1},{3,4},{4,3},{5,6},{6,5},{7,0},{0,7},{9,10},{10,9},{11,... | collective-permute-start | bytes 380936 | tf_op jit(solution)/shard_map/ppermute | solution.py:312
  15.2 0.0 copy-done.1
  15.2 0.0 copy-start
  15.2 1.6 %copy-done = f32[16,16,16,128]{3,2,1,0:T(8,128)S(1)} copy-done((f32[16,16,16,128]{3,2,1,0:T(8,128)S(1)}, f32[16,16,16,128]{3,2,1,0:T(8,128)}, u32[]{:S(2)}) %copy-start) | copy-done | bytes 2097176
  16.8 3.5 %shard_map.28 = (f32[16,256,128]{2,1,0:T(8,128)S(1)}, f32[256,128]{1,0:T(8,128)S(1)}, f32[256,128]{1,0:T(8,128)S(1)}, f32[256,128]{1,0:T(8,128)S(1)}, f32[256,12...) custom-call(f32[16,256,128]{2,1,0:T(8,128)S(1)} %bitcast.3, ...), custom_call_target="tpu_custom_call" | custom-call | flops 4294967296 | bytes 4194304 | tf_op jit(solution)/shard_map/pallas_call | solution.py:345
  20.3 0.0 collective-permute-done.ga_ref
  20.3 0.0 collective-permute-done.1.gb_ref
  20.4 0.6 %shard_map.30 = (f32[240,128]{1,0:T(8,128)S(1)}, f32[240,128]{1,0:T(8,128)S(1)}, f32[256,128]{1,0:T(8,128)S(1)}, f32[256,128]{1,0:T(8,128)S(1)}, f32[16,16,128]{2,1,0:T(8,128)S(1)}, /*index=5*/f32[16,16,128]{2,1,0:T(8,128)S(1)}) custom-call(f32[24,128]{1,0:T(8,128)S(1)} %get-tuple-element.38.lists_ref, f32[248,128]{1,0:T(8,128)S(1)} %collective-permute-done.ga_ref, ...), custom_call_target="tpu_custom_call" | custom-call | bytes 1048576 | tf_op jit(solution)/shard_map/pallas_call | solution.py:352
  21.0 5.5 %collective-permute-start.4 = (f32[240,128]{1,0:T(8,128)S(1)}, f32[240,128]{1,0:T(8,128)S(1)}, u32[]{:S(2)}, u32[]{:S(2)}) collective-permute-start(f32[240,128]{1,0:T(8,128)S(1)} %get-tuple-element.52), channel_id=1, source_target_pairs={{0,1},{1,0},{2,3},{3,2},{4,5},{5,4},{6,7},{7,6},{8,9},{9,8},{10,11... | collective-permute-start | bytes 368648 | tf_op jit(solution)/shard_map/ppermute | solution.py:312
  26.5 2.7 %collective-permute-start.5 = (f32[240,128]{1,0:T(8,128)S(1)}, f32[240,128]{1,0:T(8,128)S(1)}, u32[]{:S(2)}, u32[]{:S(2)}) collective-permute-start(f32[240,128]{1,0:T(8,128)S(1)} %get-tuple-element.53), channel_id=1, source_target_pairs={{1,2},{2,1},{3,4},{4,3},{5,6},{6,5},{7,0},{0,7},{9,10},{10,9},{11,... | collective-permute-start | bytes 368648 | tf_op jit(solution)/shard_map/ppermute | solution.py:312
  29.2 0.0 collective-permute-done.2.ga_ref
  29.2 0.0 collective-permute-done.3.gb_ref
  29.2 0.6 %shard_map.31 = (f32[240,128]{1,0:T(8,128)S(1)}, f32[240,128]{1,0:T(8,128)S(1)}, f32[256,128]{1,0:T(8,128)S(1)}, f32[256,128]{1,0:T(8,128)S(1)}, f32[16,16,128]{2,1,0:T(8,128)S(1)}, /*index=5*/f32[16,16,128]{2,1,0:T(8,128)S(1)}) custom-call(f32[24,128]{1,0:T(8,128)S(1)} %get-tuple-element.38.lists_ref, f32[248,128]{1,0:T(8,128)S(1)} %collective-permute-done.2.ga_ref, ...), custom_call_target="tpu_custom_call" | custom-call | bytes 1048576 | tf_op jit(solution)/shard_map/pallas_call | solution.py:356
  29.9 0.1 collective-permute-start.6
  30.0 0.3 collective-permute-start.7
  30.3 4.7 %shard_map.32 = (f32[16,256,128]{2,1,0:T(8,128)}, f32[256,128]{1,0:T(8,128)S(1)}, f32[256,128]{1,0:T(8,128)S(1)}, f32[256,128]{1,0:T(8,128)S(1)}, f32[256,128]{1,0:T(8,128)S(1)}) custom-call(f32[16,256,128]{2,1,0:T(8,128)S(1)} %get-tuple-element.37.field_ref, f32[24,128]{1,0:T(8,128)S(1)} %get-tuple-element.38.lists_ref, ...), custom_call_target="tpu_custom_call" | custom-call | flops 4294967296 | bytes 5242880 | tf_op jit(solution)/shard_map/pallas_call | solution.py:360
  34.9 0.0 collective-permute-done.4.gya_ref
  34.9 5.3 %collective-permute-done.5.gyb_ref = f32[240,128]{1,0:T(8,128)S(1)} collective-permute-done((f32[240,128]{1,0:T(8,128)S(1)}, f32[240,128]{1,0:T(8,128)S(1)}, u32[]{:S(2)}, u32[]{:S(2)}) %collective-permute-start.5) | collective-permute-done | bytes 122912 | tf_op jit(solution)/shard_map/ppermute | solution.py:312
  40.2 1.3 %shard_map.33 = (f32[16,16,16,128]{3,2,1,0:T(8,128)}, f32[256,128]{1,0:T(8,128)S(1)}, f32[256,128]{1,0:T(8,128)S(1)}) custom-call(f32[16,16,16,128]{3,2,1,0:T(8,128)} %bitcast.6, f32[240,128]{1,0:T(8,128)S(1)} %collective-permute-done.4.gya_ref, f32[240,128]{1,0:T(8,128)S(1)} %collective-permute-done.5.gyb_ref, ...), custom_call_target="tpu_custom_call", output_to_operand_aliasing={{0}: (0, {})} | custom-call | bytes 1048576 | tf_op jit(solution)/shard_map/pallas_call | solution.py:367
  41.5 0.0 collective-permute-done.6.gxa_ref
  41.5 0.0 collective-permute-done.7.gxb_ref
  41.5 1.0 %shard_map.34 = f32[16,16,16,128]{3,2,1,0:T(8,128)} custom-call(f32[16,16,16,128]{3,2,1,0:T(8,128)} %get-tuple-element.60.part_ref, f32[240,128]{1,0:T(8,128)S(1)} %collective-permute-done.6.gxa_ref, f32[240,128]{1,0:T(8,128)S(1)} %collective-permute-done.7.gxb_ref, f32[16,16,128]{2,1,0:T(8,128)S(1)} %get-tuple-element.63.mxa_ref, ...), custom_call_target="tpu_custom_call", output_to_operand_aliasing={{}: (0, {})} | custom-call | bytes 1048576 | tf_op jit(solution)/shard_map/pallas_call | solution.py:376
Async XLA Ops:
  0.0 15.2 %copy-start.1 = (s32[1,1,8,16]{3,2,1,0:T(8,128)S(1)}, s32[1,1,8,16]{3,2,1,0:T(8,128)}, u32[]{:S(2)}) copy-start(s32[1,1,8,16]{3,2,1,0:T(8,128)} %param.3) | copy-start | bytes 1540
  2.0 18.3 %collective-permute-start = (f32[248,128]{1,0:T(8,128)}, f32[248,128]{1,0:T(8,128)S(1)}, u32[]{:S(2)}, u32[]{:S(2)}) collective-permute-start(f32[248,128]{1,0:T(8,128)} %get-tuple-element.39), channel_id=1, source_target_pairs={{0,8},{8,0},{16,24},{24,16},{32,40},{40,32},{48,56},{56,48},{64,72... | collective-permute-start | bytes 380936 | tf_op jit(solution)/shard_map/ppermute | solution.py:312
  2.1 18.2 %collective-permute-start.1 = (f32[248,128]{1,0:T(8,128)}, f32[248,128]{1,0:T(8,128)S(1)}, u32[]{:S(2)}, u32[]{:S(2)}) collective-permute-start(f32[248,128]{1,0:T(8,128)} %get-tuple-element.40), channel_id=1, source_target_pairs={{8,16},{16,8},{24,32},{32,24},{40,48},{48,40},{56,64},{64,56},{72,... | collective-permute-start | bytes 380936 | tf_op jit(solution)/shard_map/ppermute | solution.py:312
  9.3 19.9 %collective-permute-start.2 = (f32[248,128]{1,0:T(8,128)}, f32[248,128]{1,0:T(8,128)S(1)}, u32[]{:S(2)}, u32[]{:S(2)}) collective-permute-start(f32[248,128]{1,0:T(8,128)} %get-tuple-element.45), channel_id=1, source_target_pairs={{0,1},{1,0},{2,3},{3,2},{4,5},{5,4},{6,7},{7,6},{8,9},{9,8},{10,11... | collective-permute-start | bytes 380936 | tf_op jit(solution)/shard_map/ppermute | solution.py:312
  13.8 15.4 %collective-permute-start.3 = (f32[248,128]{1,0:T(8,128)}, f32[248,128]{1,0:T(8,128)S(1)}, u32[]{:S(2)}, u32[]{:S(2)}) collective-permute-start(f32[248,128]{1,0:T(8,128)} %get-tuple-element.46), channel_id=1, source_target_pairs={{1,2},{2,1},{3,4},{4,3},{5,6},{6,5},{7,0},{0,7},{9,10},{10,9},{11,... | collective-permute-start | bytes 380936 | tf_op jit(solution)/shard_map/ppermute | solution.py:312
  15.2 1.6 %copy-start = (f32[16,16,16,128]{3,2,1,0:T(8,128)S(1)}, f32[16,16,16,128]{3,2,1,0:T(8,128)}, u32[]{:S(2)}) copy-start(f32[16,16,16,128]{3,2,1,0:T(8,128)} %field_ref.1) | copy-start | bytes 6291460
  21.0 13.9 %collective-permute-start.4 = (f32[240,128]{1,0:T(8,128)S(1)}, f32[240,128]{1,0:T(8,128)S(1)}, u32[]{:S(2)}, u32[]{:S(2)}) collective-permute-start(f32[240,128]{1,0:T(8,128)S(1)} %get-tuple-element.52), channel_id=1, source_target_pairs={{0,1},{1,0},{2,3},{3,2},{4,5},{5,4},{6,7},{7,6},{8,9},{9,8},{10,11... | collective-permute-start | bytes 368648 | tf_op jit(solution)/shard_map/ppermute | solution.py:312
  26.5 13.7 %collective-permute-start.5 = (f32[240,128]{1,0:T(8,128)S(1)}, f32[240,128]{1,0:T(8,128)S(1)}, u32[]{:S(2)}, u32[]{:S(2)}) collective-permute-start(f32[240,128]{1,0:T(8,128)S(1)} %get-tuple-element.53), channel_id=1, source_target_pairs={{1,2},{2,1},{3,4},{4,3},{5,6},{6,5},{7,0},{0,7},{9,10},{10,9},{11,... | collective-permute-start | bytes 368648 | tf_op jit(solution)/shard_map/ppermute | solution.py:312
  29.9 11.6 %collective-permute-start.6 = (f32[240,128]{1,0:T(8,128)S(1)}, f32[240,128]{1,0:T(8,128)S(1)}, u32[]{:S(2)}, u32[]{:S(2)}) collective-permute-start(f32[240,128]{1,0:T(8,128)S(1)} %get-tuple-element.61), channel_id=1, source_target_pairs={{0,8},{8,0},{16,24},{24,16},{32,40},{40,32},{48,56},{56,48},{64,72... | collective-permute-start | bytes 368648 | tf_op jit(solution)/shard_map/ppermute | solution.py:312
  30.0 11.5 %collective-permute-start.7 = (f32[240,128]{1,0:T(8,128)S(1)}, f32[240,128]{1,0:T(8,128)S(1)}, u32[]{:S(2)}, u32[]{:S(2)}) collective-permute-start(f32[240,128]{1,0:T(8,128)S(1)} %get-tuple-element.62), channel_id=1, source_target_pairs={{8,16},{16,8},{24,32},{32,24},{40,48},{48,40},{56,64},{64,56},{72,... | collective-permute-start | bytes 368648 | tf_op jit(solution)/shard_map/ppermute | solution.py:312

commit v4 on v2

--- a/solution.py
+++ b/solution.py
@@ -243,39 +243,47 @@
     take_faces(out_ref, (xa_ref, xb_ref), (ya_ref, yb_ref))
 
 
+def last_y_kernel(
+    gya_ref, gyb_ref, mya_ref, myb_ref, oya_ref, oyb_ref, fya_ref, fyb_ref, ya_ref, yb_ref, cya_ref, cyb_ref
+):
+    for got, match, own, face, ref, out in (
+        (gya_ref, mya_ref, oya_ref, fya_ref, ya_ref, cya_ref),
+        (gyb_ref, myb_ref, oyb_ref, fyb_ref, yb_ref, cyb_ref),
+    ):
+        remap(got, match, out, own)
+        ref[...] = out[...] + face[...]
+
+
 def last_kernel(
-    part_ref, gxa_ref, gxb_ref, gya_ref, gyb_ref, mxa_ref, mxb_ref, mya_ref, myb_ref, oya_ref, oyb_ref,
-    fxa_ref, fxb_ref, fya_ref, fyb_ref, out_ref, cxa_ref, cxb_ref, face_ref, planes_ref, rows_ref, sems,
+    part_ref, gxa_ref, gxb_ref, mxa_ref, mxb_ref, fxa_ref, fxb_ref, ya_ref, yb_ref, cya_ref, cyb_ref,
+    out_ref, face_ref, planes_ref, rows_ref, sems,
 ):
     del part_ref
+    odd = lax.axis_index("gy") & 1
+    for n, ref in enumerate((ya_ref, yb_ref)):
+        rows_ref[(odd + 1 + n) % 2] = ref[...].reshape(SLOTS, TILE, 1, NZ)
+    rows = [
+        pltpu.make_async_copy(rows_ref.at[i], out_ref.at[:, :, pl.ds(y, 1), :], sems.at[i])
+        for i, y in enumerate((0, TILE - 1))
+    ]
+    for copy in rows:
+        copy.start()
     odd = lax.axis_index("gx") & 1
-    for n, (got, match, face, out) in enumerate(
-        ((gxa_ref, mxa_ref, fxa_ref, cxa_ref), (gxb_ref, mxb_ref, fxb_ref, cxb_ref))
+    for n, (got, match, face, x) in enumerate(
+        zip((gxa_ref, gxb_ref), (mxa_ref, mxb_ref), (fxa_ref, fxb_ref), sides("gx"))
     ):
-        remap(got, match, out)
-        planes_ref[(odd + 1 + n) % 2] = (out[...] + face[...]).reshape(SLOTS, 1, TILE, NZ)
+        remap(got, match, face_ref)
+        add_rows(face_ref, x, (cya_ref, cyb_ref), sides("gy"))
+        planes_ref[(odd + 1 + n) % 2] = (face_ref[...] + face[...]).reshape(SLOTS, 1, TILE, NZ)
+    for copy in rows:
+        copy.wait()
     planes = [
-        pltpu.make_async_copy(planes_ref.at[i], out_ref.at[:, pl.ds(x, 1), :, :], sems.at[i])
+        pltpu.make_async_copy(planes_ref.at[i], out_ref.at[:, pl.ds(x, 1), :, :], sems.at[2 + i])
         for i, x in enumerate((0, TILE - 1))
     ]
     for copy in planes:
         copy.start()
-    odd = lax.axis_index("gy") & 1
-    for n, (got, match, own, face, y) in enumerate(zip(
-        (gya_ref, gyb_ref), (mya_ref, myb_ref), (oya_ref, oyb_ref), (fya_ref, fyb_ref), sides("gy")
-    )):
-        remap(got, match, face_ref, own)
-        add_rows(face_ref, y, (cxa_ref, cxb_ref), sides("gx"))
-        rows_ref[(odd + 1 + n) % 2] = (face_ref[...] + face[...]).reshape(SLOTS, TILE, 1, NZ)
     for copy in planes:
-        copy.wait()
-    rows = [
-        pltpu.make_async_copy(rows_ref.at[i], out_ref.at[:, :, pl.ds(y, 1), :], sems.at[2 + i])
-        for i, y in enumerate((0, TILE - 1))
-    ]
-    for copy in rows:
-        copy.start()
-    for copy in rows:
         copy.wait()
 
 
@@ -356,24 +364,23 @@
         flops=4 << 30,
         bytes_accessed=5 << 20,
     )(part, lists, cxa, cxb, cya, cyb)
+    fya, fyb, cya, cyb = call(last_y_kernel, [SIDE] * 4, bytes_accessed=1 << 20)(
+        gpya, gpyb, mya, myb, oya, oyb, fya, fyb
+    )
     (out,) = call(
         last_kernel,
         [phase_fields.shape],
         [
             (SIDE, F32),
-            (SIDE, F32),
-            (SIDE, F32),
             ((2, SLOTS, 1, TILE, NZ), F32),
             ((2, SLOTS, TILE, 1, NZ), F32),
             pltpu.SemaphoreType.DMA((4,)),
         ],
-        bytes_accessed=5 << 20,
-        in_specs=[ANYWHERE] + [HERE] * 14,
+        bytes_accessed=1 << 20,
+        in_specs=[ANYWHERE] + [HERE] * 10,
         out_specs=[ANYWHERE],
         input_output_aliases={0: 0},
-    )(
-        part.reshape(phase_fields.shape), gpxa, gpxb, gpya, gpyb, mxa, mxb, mya, myb, oya, oyb, fxa, fxb, fya, fyb
-    )
+    )(part.reshape(phase_fields.shape), gpxa, gpxb, mxa, mxb, fxa, fxb, fya, fyb, cya, cyb)
     return out
 
 

time: 43.2 us -> 43 us (level)
    pallas_call x1 -> x2, Pallas kernels: 1.71 us -> 1.96 us  [the longest x1 1.59 us: shards(): call(last_kernel, [phase_fields.shape], [(SIDE, F32), ((2, SLOTS, 1, TILE...]
  transfers between devices with their start and end apart: 8 -> 8, of which waited for: 2 -> 2; matrix products, arithmetic and copies ran while one was open for 0% -> 0% of each run, Pallas kernels for 22% -> 23%
where the time goes in v4:
time: 43 us; the launch traced here: 42.9 us
  starting transfers between devices  21.8 us (51%)
  Pallas kernels  13.5 us (31%)
  waiting for transfers between devices  5.85 us (14%)
  local copies, waits for them, and re-layouts  1.59 us (4%)
    ppermute x8, starting transfers between devices, exchange(): return lax.ppermute(value, axis, pairs(lax.axis_size(axis), which))  21.8 us
    ppermute x8, waiting for transfers between devices, exchange(): return lax.ppermute(value, axis, pairs(lax.axis_size(axis), which))  5.85 us
    pallas_call x1, Pallas kernels, shards(): call(second_kernel, [WHOLE] + [SIDE] * 4, [(WHOLE, F32)] + STEP_SCRATCH,...  4.67 us
    pallas_call x1, Pallas kernels, shards(): call(first_kernel, [WHOLE] + [SIDE] * 6 + [LISTS], STEP_SCRATCH, flops=4...  3.52 us
    pallas_call x1, Pallas kernels, shards(): call(pack_kernel, [FIRST] * 4, [((2, SLOTS, 1, TILE, NZ), F32), ((2, SLOT...  2.02 us
    unnamed x4, local copies, waits for them, and re-layouts  1.59 us
    pallas_call x1, Pallas kernels, shards(): call(last_kernel, [phase_fields.shape], [(SIDE, F32), ((2, SLOTS, 1, TILE...  1.59 us
  transfers between devices with their start and end apart: 8, of which 2 were waited for; matrix products, arithmetic and copies ran while one was open for 0% of the time, Pallas kernels for 23%

profile of v4, /device:TPU:2, one launch (start us, length us, event | category | flops | bytes accessed | tf_op | source)
XLA Modules:
  0.0 42.9 jit_solution(7829112392691846801)
XLA Ops:
  0.0 0.0 copy-start.1
  0.0 2.0 %shard_map.29 = (f32[248,128]{1,0:T(8,128)}, f32[248,128]{1,0:T(8,128)}, f32[248,128]{1,0:T(8,128)}, f32[248,128]{1,0:T(8,128)}) custom-call(f32[16,16,16,128]{3,2,1,0:T(8,128)} %field_ref.1, s32[8,16]{1,0:T(8,128)} %bitcast.4), custom_call_target="tpu_custom_call" | custom-call | bytes 3145728 | tf_op jit(solution)/shard_map/pallas_call | solution.py:329
  2.0 0.1 collective-permute-start
  2.1 7.2 %collective-permute-start.1 = (f32[248,128]{1,0:T(8,128)}, f32[248,128]{1,0:T(8,128)S(1)}, u32[]{:S(2)}, u32[]{:S(2)}) collective-permute-start(f32[248,128]{1,0:T(8,128)} %get-tuple-element.41), channel_id=1, source_target_pairs={{8,16},{16,8},{24,32},{32,24},{40,48},{48,40},{56,64},{64,56},{72,... | collective-permute-start | bytes 380936 | tf_op jit(solution)/shard_map/ppermute | solution.py:312
  9.3 4.5 %collective-permute-start.2 = (f32[248,128]{1,0:T(8,128)}, f32[248,128]{1,0:T(8,128)S(1)}, u32[]{:S(2)}, u32[]{:S(2)}) collective-permute-start(f32[248,128]{1,0:T(8,128)} %get-tuple-element.46), channel_id=1, source_target_pairs={{0,1},{1,0},{2,3},{3,2},{4,5},{5,4},{6,7},{7,6},{8,9},{9,8},{10,11... | collective-permute-start | bytes 380936 | tf_op jit(solution)/shard_map/ppermute | solution.py:312
  13.8 1.4 %collective-permute-start.3 = (f32[248,128]{1,0:T(8,128)}, f32[248,128]{1,0:T(8,128)S(1)}, u32[]{:S(2)}, u32[]{:S(2)}) collective-permute-start(f32[248,128]{1,0:T(8,128)} %get-tuple-element.47), channel_id=1, source_target_pairs={{1,2},{2,1},{3,4},{4,3},{5,6},{6,5},{7,0},{0,7},{9,10},{10,9},{11,... | collective-permute-start | bytes 380936 | tf_op jit(solution)/shard_map/ppermute | solution.py:312
  15.2 0.0 copy-done.1
  15.2 0.0 copy-start
  15.2 1.6 %copy-done = f32[16,16,16,128]{3,2,1,0:T(8,128)S(1)} copy-done((f32[16,16,16,128]{3,2,1,0:T(8,128)S(1)}, f32[16,16,16,128]{3,2,1,0:T(8,128)}, u32[]{:S(2)}) %copy-start) | copy-done | bytes 2097176
  16.8 3.5 %shard_map.28 = (f32[16,256,128]{2,1,0:T(8,128)S(1)}, f32[256,128]{1,0:T(8,128)S(1)}, f32[256,128]{1,0:T(8,128)S(1)}, f32[256,128]{1,0:T(8,128)S(1)}, f32[256,12...) custom-call(f32[16,256,128]{2,1,0:T(8,128)S(1)} %bitcast.3, ...), custom_call_target="tpu_custom_call" | custom-call | flops 4294967296 | bytes 4194304 | tf_op jit(solution)/shard_map/pallas_call | solution.py:345
  20.3 0.0 collective-permute-done.ga_ref
  20.3 0.0 collective-permute-done.1.gb_ref
  20.4 0.6 %shard_map.30 = (f32[240,128]{1,0:T(8,128)S(1)}, f32[240,128]{1,0:T(8,128)S(1)}, f32[256,128]{1,0:T(8,128)S(1)}, f32[256,128]{1,0:T(8,128)S(1)}, f32[16,16,128]{2,1,0:T(8,128)S(1)}, /*index=5*/f32[16,16,128]{2,1,0:T(8,128)S(1)}) custom-call(f32[24,128]{1,0:T(8,128)S(1)} %get-tuple-element.39.lists_ref, f32[248,128]{1,0:T(8,128)S(1)} %collective-permute-done.ga_ref, ...), custom_call_target="tpu_custom_call" | custom-call | bytes 1048576 | tf_op jit(solution)/shard_map/pallas_call | solution.py:352
  21.0 5.5 %collective-permute-start.6 = (f32[240,128]{1,0:T(8,128)S(1)}, f32[240,128]{1,0:T(8,128)S(1)}, u32[]{:S(2)}, u32[]{:S(2)}) collective-permute-start(f32[240,128]{1,0:T(8,128)S(1)} %get-tuple-element.59), channel_id=1, source_target_pairs={{0,1},{1,0},{2,3},{3,2},{4,5},{5,4},{6,7},{7,6},{8,9},{9,8},{10,11... | collective-permute-start | bytes 368648 | tf_op jit(solution)/shard_map/ppermute | solution.py:312
  26.5 2.7 %collective-permute-start.7 = (f32[240,128]{1,0:T(8,128)S(1)}, f32[240,128]{1,0:T(8,128)S(1)}, u32[]{:S(2)}, u32[]{:S(2)}) collective-permute-start(f32[240,128]{1,0:T(8,128)S(1)} %get-tuple-element.60), channel_id=1, source_target_pairs={{1,2},{2,1},{3,4},{4,3},{5,6},{6,5},{7,0},{0,7},{9,10},{10,9},{11,... | collective-permute-start | bytes 368648 | tf_op jit(solution)/shard_map/ppermute | solution.py:312
  29.2 0.0 collective-permute-done.2.ga_ref
  29.2 0.0 collective-permute-done.3.gb_ref
  29.2 0.7 %shard_map.31 = (f32[240,128]{1,0:T(8,128)S(1)}, f32[240,128]{1,0:T(8,128)S(1)}, f32[256,128]{1,0:T(8,128)S(1)}, f32[256,128]{1,0:T(8,128)S(1)}, f32[16,16,128]{2,1,0:T(8,128)S(1)}, /*index=5*/f32[16,16,128]{2,1,0:T(8,128)S(1)}) custom-call(f32[24,128]{1,0:T(8,128)S(1)} %get-tuple-element.39.lists_ref, f32[248,128]{1,0:T(8,128)S(1)} %collective-permute-done.2.ga_ref, ...), custom_call_target="tpu_custom_call" | custom-call | bytes 1048576 | tf_op jit(solution)/shard_map/pallas_call | solution.py:356
  29.9 0.1 collective-permute-start.4
  30.0 0.3 collective-permute-start.5
  30.3 4.7 %shard_map.32 = (f32[16,256,128]{2,1,0:T(8,128)}, f32[256,128]{1,0:T(8,128)S(1)}, f32[256,128]{1,0:T(8,128)S(1)}, f32[256,128]{1,0:T(8,128)S(1)}, f32[256,128]{1,0:T(8,128)S(1)}) custom-call(f32[16,256,128]{2,1,0:T(8,128)S(1)} %get-tuple-element.38.field_ref, f32[24,128]{1,0:T(8,128)S(1)} %get-tuple-element.39.lists_ref, ...), custom_call_target="tpu_custom_call" | custom-call | flops 4294967296 | bytes 5242880 | tf_op jit(solution)/shard_map/pallas_call | solution.py:360
  34.9 0.0 collective-permute-done.6.gya_ref
  34.9 5.3 %collective-permute-done.7.gyb_ref = f32[240,128]{1,0:T(8,128)S(1)} collective-permute-done((f32[240,128]{1,0:T(8,128)S(1)}, f32[240,128]{1,0:T(8,128)S(1)}, u32[]{:S(2)}, u32[]{:S(2)}) %collective-permute-start.7) | collective-permute-done | bytes 122912 | tf_op jit(solution)/shard_map/ppermute | solution.py:312
  40.2 0.4 shard_map.33
  40.6 0.0 collective-permute-done.4.gxa_ref
  40.6 0.6 %collective-permute-done.5.gxb_ref = f32[240,128]{1,0:T(8,128)S(1)} collective-permute-done((f32[240,128]{1,0:T(8,128)S(1)}, f32[240,128]{1,0:T(8,128)S(1)}, u32[]{:S(2)}, u32[]{:S(2)}) %collective-permute-start.5) | collective-permute-done | bytes 122912 | tf_op jit(solution)/shard_map/ppermute | solution.py:312
  41.2 1.6 %shard_map.34 = f32[16,16,16,128]{3,2,1,0:T(8,128)} custom-call(f32[16,16,16,128]{3,2,1,0:T(8,128)} %bitcast.6, f32[240,128]{1,0:T(8,128)S(1)} %collective-permute-done.4.gxa_ref, f32[240,128]{1,0:T(8,128)S(1)} %collective-permute-done.5.gxb_ref, f32[16,16,128]{2,1,0:T(8,128)S(1)} %get-tuple-element.55.mxa_ref, ...), custom_call_target="tpu_custom_call", output_to_operand_aliasing={{}: (0, {})} | custom-call | bytes 1048576 | tf_op jit(solution)/shard_map/pallas_call | solution.py:370
Async XLA Ops:
  0.0 15.2 %copy-start.1 = (s32[1,1,8,16]{3,2,1,0:T(8,128)S(1)}, s32[1,1,8,16]{3,2,1,0:T(8,128)}, u32[]{:S(2)}) copy-start(s32[1,1,8,16]{3,2,1,0:T(8,128)} %param.3) | copy-start | bytes 1540
  2.0 18.3 %collective-permute-start = (f32[248,128]{1,0:T(8,128)}, f32[248,128]{1,0:T(8,128)S(1)}, u32[]{:S(2)}, u32[]{:S(2)}) collective-permute-start(f32[248,128]{1,0:T(8,128)} %get-tuple-element.40), channel_id=1, source_target_pairs={{0,8},{8,0},{16,24},{24,16},{32,40},{40,32},{48,56},{56,48},{64,72... | collective-permute-start | bytes 380936 | tf_op jit(solution)/shard_map/ppermute | solution.py:312
  2.1 18.2 %collective-permute-start.1 = (f32[248,128]{1,0:T(8,128)}, f32[248,128]{1,0:T(8,128)S(1)}, u32[]{:S(2)}, u32[]{:S(2)}) collective-permute-start(f32[248,128]{1,0:T(8,128)} %get-tuple-element.41), channel_id=1, source_target_pairs={{8,16},{16,8},{24,32},{32,24},{40,48},{48,40},{56,64},{64,56},{72,... | collective-permute-start | bytes 380936 | tf_op jit(solution)/shard_map/ppermute | solution.py:312
  9.3 19.9 %collective-permute-start.2 = (f32[248,128]{1,0:T(8,128)}, f32[248,128]{1,0:T(8,128)S(1)}, u32[]{:S(2)}, u32[]{:S(2)}) collective-permute-start(f32[248,128]{1,0:T(8,128)} %get-tuple-element.46), channel_id=1, source_target_pairs={{0,1},{1,0},{2,3},{3,2},{4,5},{5,4},{6,7},{7,6},{8,9},{9,8},{10,11... | collective-permute-start | bytes 380936 | tf_op jit(solution)/shard_map/ppermute | solution.py:312
  13.8 15.4 %collective-permute-start.3 = (f32[248,128]{1,0:T(8,128)}, f32[248,128]{1,0:T(8,128)S(1)}, u32[]{:S(2)}, u32[]{:S(2)}) collective-permute-start(f32[248,128]{1,0:T(8,128)} %get-tuple-element.47), channel_id=1, source_target_pairs={{1,2},{2,1},{3,4},{4,3},{5,6},{6,5},{7,0},{0,7},{9,10},{10,9},{11,... | collective-permute-start | bytes 380936 | tf_op jit(solution)/shard_map/ppermute | solution.py:312
  15.2 1.6 %copy-start = (f32[16,16,16,128]{3,2,1,0:T(8,128)S(1)}, f32[16,16,16,128]{3,2,1,0:T(8,128)}, u32[]{:S(2)}) copy-start(f32[16,16,16,128]{3,2,1,0:T(8,128)} %field_ref.1) | copy-start | bytes 6291460
  21.0 13.9 %collective-permute-start.6 = (f32[240,128]{1,0:T(8,128)S(1)}, f32[240,128]{1,0:T(8,128)S(1)}, u32[]{:S(2)}, u32[]{:S(2)}) collective-permute-start(f32[240,128]{1,0:T(8,128)S(1)} %get-tuple-element.59), channel_id=1, source_target_pairs={{0,1},{1,0},{2,3},{3,2},{4,5},{5,4},{6,7},{7,6},{8,9},{9,8},{10,11... | collective-permute-start | bytes 368648 | tf_op jit(solution)/shard_map/ppermute | solution.py:312
  26.5 13.7 %collective-permute-start.7 = (f32[240,128]{1,0:T(8,128)S(1)}, f32[240,128]{1,0:T(8,128)S(1)}, u32[]{:S(2)}, u32[]{:S(2)}) collective-permute-start(f32[240,128]{1,0:T(8,128)S(1)} %get-tuple-element.60), channel_id=1, source_target_pairs={{1,2},{2,1},{3,4},{4,3},{5,6},{6,5},{7,0},{0,7},{9,10},{10,9},{11,... | collective-permute-start | bytes 368648 | tf_op jit(solution)/shard_map/ppermute | solution.py:312
  29.9 10.7 %collective-permute-start.4 = (f32[240,128]{1,0:T(8,128)S(1)}, f32[240,128]{1,0:T(8,128)S(1)}, u32[]{:S(2)}, u32[]{:S(2)}) collective-permute-start(f32[240,128]{1,0:T(8,128)S(1)} %get-tuple-element.53), channel_id=1, source_target_pairs={{0,8},{8,0},{16,24},{24,16},{32,40},{40,32},{48,56},{56,48},{64,72... | collective-permute-start | bytes 368648 | tf_op jit(solution)/shard_map/ppermute | solution.py:312
  30.0 11.2 %collective-permute-start.5 = (f32[240,128]{1,0:T(8,128)S(1)}, f32[240,128]{1,0:T(8,128)S(1)}, u32[]{:S(2)}, u32[]{:S(2)}) collective-permute-start(f32[240,128]{1,0:T(8,128)S(1)} %get-tuple-element.54), channel_id=1, source_target_pairs={{8,16},{16,8},{24,32},{32,24},{40,48},{48,40},{56,64},{64,56},{72,... | collective-permute-start | bytes 368648 | tf_op jit(solution)/shard_map/ppermute | solution.py:312

commit v5 on v4

--- a/solution.py
+++ b/solution.py
@@ -193,13 +193,12 @@
 
 
 def first_kernel(
-    field_ref, ids_ref, out_ref, xa_ref, xb_ref, ya_ref, yb_ref, oya_ref, oyb_ref, lists_ref, halves_ref, edge_ref
+    field_ref, ids_ref, out_ref, xa_ref, xb_ref, ya_ref, yb_ref, lists_ref, halves_ref, edge_ref
 ):
     flat = flat_ids(ids_ref[...])
     lists_ref[:SLOTS, :] = lane_ids(flat)
     lists_ref[SLOTS:, :] = jnp.broadcast_to(flat, (8, NZ))
     step(field_ref, lists_ref, out_ref, halves_ref, edge_ref)
-    take_faces(field_ref, (), (oya_ref, oyb_ref))
     take_faces(out_ref, (xa_ref, xb_ref), (ya_ref, yb_ref))
 
 
@@ -234,9 +233,10 @@
 
 
 def second_kernel(
-    field_ref, lists_ref, cxa_ref, cxb_ref, cya_ref, cyb_ref,
-    out_ref, xa_ref, xb_ref, ya_ref, yb_ref, state_ref, halves_ref, edge_ref,
-):
+    field_ref, start_ref, lists_ref, cxa_ref, cxb_ref, cya_ref, cyb_ref,
+    out_ref, xa_ref, xb_ref, ya_ref, yb_ref, oya_ref, oyb_ref, state_ref, halves_ref, edge_ref,
+):
+    take_faces(start_ref, (), (oya_ref, oyb_ref))
     state_ref[...] = field_ref[...]
     add_faces(state_ref, (cxa_ref, cxb_ref), (cya_ref, cyb_ref), sides("gx"), sides("gy"))
     step(state_ref, lists_ref, out_ref, halves_ref, edge_ref)
@@ -342,9 +342,9 @@
     )(phase_fields, ids)
     gxa, gxb = exchange(sxa, "gx", 0), exchange(sxb, "gx", 1)
     gya, gyb = exchange(sya, "gy", 0), exchange(syb, "gy", 1)
-    part, pxa, pxb, pya, pyb, oya, oyb, lists = call(
+    part, pxa, pxb, pya, pyb, lists = call(
         first_kernel,
-        [WHOLE] + [SIDE] * 6 + [LISTS],
+        [WHOLE] + [SIDE] * 4 + [LISTS],
         STEP_SCRATCH,
         flops=4 << 30,
         bytes_accessed=4 << 20,
@@ -357,13 +357,13 @@
         y_kernel, [SECOND] * 2 + [SIDE] * 2 + [MATCH] * 2, [(SIDE, F32)], bytes_accessed=1 << 20
     )(lists, gya, gyb, pxa, pxb, cxa, cxb)
     gpxa, gpxb = exchange(txa, "gx", 0), exchange(txb, "gx", 1)
-    part, fxa, fxb, fya, fyb = call(
+    part, fxa, fxb, fya, fyb, oya, oyb = call(
         second_kernel,
-        [WHOLE] + [SIDE] * 4,
+        [WHOLE] + [SIDE] * 6,
         [(WHOLE, F32)] + STEP_SCRATCH,
         flops=4 << 30,
         bytes_accessed=5 << 20,
-    )(part, lists, cxa, cxb, cya, cyb)
+    )(part, field, lists, cxa, cxb, cya, cyb)
     fya, fyb, cya, cyb = call(last_y_kernel, [SIDE] * 4, bytes_accessed=1 << 20)(
         gpya, gpyb, mya, myb, oya, oyb, fya, fyb
     )

time: 43 us -> 43 us (level)
    unnamed x4 -> x6, local copies, waits for them, and re-layouts: 1.59 us -> 1.6 us
where the time goes in v5:
time: 43 us; the launch traced here: 42.9 us
  starting transfers between devices  21.8 us (51%)
  Pallas kernels  13.4 us (31%)
  waiting for transfers between devices  5.86 us (14%)
  local copies, waits for them, and re-layouts  1.6 us (4%)
    ppermute x8, starting transfers between devices, exchange(): return lax.ppermute(value, axis, pairs(lax.axis_size(axis), which))  21.8 us
    ppermute x8, waiting for transfers between devices, exchange(): return lax.ppermute(value, axis, pairs(lax.axis_size(axis), which))  5.86 us
    pallas_call x1, Pallas kernels, shards(): call(second_kernel, [WHOLE] + [SIDE] * 6, [(WHOLE, F32)] + STEP_SCRATCH,...  4.8 us
    pallas_call x1, Pallas kernels, shards(): call(first_kernel, [WHOLE] + [SIDE] * 4 + [LISTS], STEP_SCRATCH, flops=4...  3.41 us
    pallas_call x1, Pallas kernels, shards(): call(pack_kernel, [FIRST] * 4, [((2, SLOTS, 1, TILE, NZ), F32), ((2, SLOT...  2.01 us
    unnamed x6, local copies, waits for them, and re-layouts  1.6 us
    pallas_call x1, Pallas kernels, shards(): call(last_kernel, [phase_fields.shape], [(SIDE, F32), ((2, SLOTS, 1, TILE...  1.59 us
  transfers between devices with their start and end apart: 8, of which 2 were waited for; matrix products, arithmetic and copies ran while one was open for 0% of the time, Pallas kernels for 23%

profile of v5, /device:TPU:2, one launch (start us, length us, event | category | flops | bytes accessed | tf_op | source)
XLA Modules:
  0.0 42.9 jit_solution(14976920294434633693)
XLA Ops:
  0.0 0.0 copy-start.2
  0.0 2.0 %shard_map.29 = (f32[248,128]{1,0:T(8,128)}, f32[248,128]{1,0:T(8,128)}, f32[248,128]{1,0:T(8,128)}, f32[248,128]{1,0:T(8,128)}) custom-call(f32[16,16,16,128]{3,2,1,0:T(8,128)} %field_ref.1, s32[8,16]{1,0:T(8,128)} %bitcast.5), custom_call_target="tpu_custom_call" | custom-call | bytes 3145728 | tf_op jit(solution)/shard_map/pallas_call | solution.py:329
  2.0 0.1 collective-permute-start
  2.1 7.2 %collective-permute-start.1 = (f32[248,128]{1,0:T(8,128)}, f32[248,128]{1,0:T(8,128)S(1)}, u32[]{:S(2)}, u32[]{:S(2)}) collective-permute-start(f32[248,128]{1,0:T(8,128)} %get-tuple-element.41), channel_id=1, source_target_pairs={{8,16},{16,8},{24,32},{32,24},{40,48},{48,40},{56,64},{64,56},{72,... | collective-permute-start | bytes 380936 | tf_op jit(solution)/shard_map/ppermute | solution.py:312
  9.3 4.5 %collective-permute-start.2 = (f32[248,128]{1,0:T(8,128)}, f32[248,128]{1,0:T(8,128)S(1)}, u32[]{:S(2)}, u32[]{:S(2)}) collective-permute-start(f32[248,128]{1,0:T(8,128)} %get-tuple-element.46), channel_id=1, source_target_pairs={{0,1},{1,0},{2,3},{3,2},{4,5},{5,4},{6,7},{7,6},{8,9},{9,8},{10,11... | collective-permute-start | bytes 380936 | tf_op jit(solution)/shard_map/ppermute | solution.py:312
  13.8 1.4 %collective-permute-start.3 = (f32[248,128]{1,0:T(8,128)}, f32[248,128]{1,0:T(8,128)S(1)}, u32[]{:S(2)}, u32[]{:S(2)}) collective-permute-start(f32[248,128]{1,0:T(8,128)} %get-tuple-element.47), channel_id=1, source_target_pairs={{1,2},{2,1},{3,4},{4,3},{5,6},{6,5},{7,0},{0,7},{9,10},{10,9},{11,... | collective-permute-start | bytes 380936 | tf_op jit(solution)/shard_map/ppermute | solution.py:312
  15.2 0.0 copy-done.2
  15.2 0.0 copy-start
  15.2 1.6 %copy-done = f32[16,16,16,128]{3,2,1,0:T(8,128)S(1)} copy-done((f32[16,16,16,128]{3,2,1,0:T(8,128)S(1)}, f32[16,16,16,128]{3,2,1,0:T(8,128)}, u32[]{:S(2)}) %copy-start) | copy-done | bytes 2097176
  16.8 0.0 copy-start.1
  16.8 3.4 %shard_map.28 = (f32[16,256,128]{2,1,0:T(8,128)S(1)}, f32[256,128]{1,0:T(8,128)S(1)}, f32[256,128]{1,0:T(8,128)S(1)}, f32[256,128]{1,0:T(8,128)S(1)}, f32[256,128]{1,0:T(8,128)S(1)}, /*index=5*/f32[24,128]{1,0:T(8,128)S(1)}) custom-call(f32[16,256,128]{2,1,0:T(8,128)S(1)} %bitcast.3, s32[8,16]{1,0:T(8,128)S(1)} %bitcast.6), custom_call_target="tpu_custom_call" | custom-call | flops 4294967296 | bytes 4194304 | tf_op jit(solution)/shard_map/pallas_call | solution.py:345
  20.2 0.0 collective-permute-done.ga_ref
  20.2 0.0 collective-permute-done.1.gb_ref
  20.2 0.6 %shard_map.30 = (f32[240,128]{1,0:T(8,128)S(1)}, f32[240,128]{1,0:T(8,128)S(1)}, f32[256,128]{1,0:T(8,128)S(1)}, f32[256,128]{1,0:T(8,128)S(1)}, f32[16,16,128]{2,1,0:T(8,128)S(1)}, /*index=5*/f32[16,16,128]{2,1,0:T(8,128)S(1)}) custom-call(f32[24,128]{1,0:T(8,128)S(1)} %get-tuple-element.39.lists_ref, f32[248,128]{1,0:T(8,128)S(1)} %collective-permute-done.ga_ref, ...), custom_call_target="tpu_custom_call" | custom-call | bytes 1048576 | tf_op jit(solution)/shard_map/pallas_call | solution.py:352
  20.9 5.5 %collective-permute-start.6 = (f32[240,128]{1,0:T(8,128)S(1)}, f32[240,128]{1,0:T(8,128)S(1)}, u32[]{:S(2)}, u32[]{:S(2)}) collective-permute-start(f32[240,128]{1,0:T(8,128)S(1)} %get-tuple-element.59), channel_id=1, source_target_pairs={{0,1},{1,0},{2,3},{3,2},{4,5},{5,4},{6,7},{7,6},{8,9},{9,8},{10,11... | collective-permute-start | bytes 368648 | tf_op jit(solution)/shard_map/ppermute | solution.py:312
  26.4 2.7 %collective-permute-start.7 = (f32[240,128]{1,0:T(8,128)S(1)}, f32[240,128]{1,0:T(8,128)S(1)}, u32[]{:S(2)}, u32[]{:S(2)}) collective-permute-start(f32[240,128]{1,0:T(8,128)S(1)} %get-tuple-element.60), channel_id=1, source_target_pairs={{1,2},{2,1},{3,4},{4,3},{5,6},{6,5},{7,0},{0,7},{9,10},{10,9},{11,... | collective-permute-start | bytes 368648 | tf_op jit(solution)/shard_map/ppermute | solution.py:312
  29.1 0.0 collective-permute-done.2.ga_ref
  29.1 0.0 collective-permute-done.3.gb_ref
  29.1 0.6 %shard_map.31 = (f32[240,128]{1,0:T(8,128)S(1)}, f32[240,128]{1,0:T(8,128)S(1)}, f32[256,128]{1,0:T(8,128)S(1)}, f32[256,128]{1,0:T(8,128)S(1)}, f32[16,16,128]{2,1,0:T(8,128)S(1)}, /*index=5*/f32[16,16,128]{2,1,0:T(8,128)S(1)}) custom-call(f32[24,128]{1,0:T(8,128)S(1)} %get-tuple-element.39.lists_ref, f32[248,128]{1,0:T(8,128)S(1)} %collective-permute-done.2.ga_ref, ...), custom_call_target="tpu_custom_call" | custom-call | bytes 1048576 | tf_op jit(solution)/shard_map/pallas_call | solution.py:356
  29.7 0.1 collective-permute-start.4
  29.8 0.3 collective-permute-start.5
  30.1 0.0 copy-done.1
  30.1 4.8 %shard_map.32 = (f32[16,256,128]{2,1,0:T(8,128)}, f32[256,128]{1,0:T(8,128)S(1)}, f32[256,128]{1,0:T(8,128)S(1)}, f32[256,128]{1,0:T(8,128)S(1)}, f32[256,128]{1...) custom-call(f32[16,256,128]{2,1,0:T(8,128)S(1)} %get-tuple-element.38.field_ref, ...), custom_call_target="tpu_custom_call" | custom-call | flops 4294967296 | bytes 5242880 | tf_op jit(solution)/shard_map/pallas_call | solution.py:360
  34.9 0.0 collective-permute-done.6.gya_ref
  34.9 5.3 %collective-permute-done.7.gyb_ref = f32[240,128]{1,0:T(8,128)S(1)} collective-permute-done((f32[240,128]{1,0:T(8,128)S(1)}, f32[240,128]{1,0:T(8,128)S(1)}, u32[]{:S(2)}, u32[]{:S(2)}) %collective-permute-start.7) | collective-permute-done | bytes 122912 | tf_op jit(solution)/shard_map/ppermute | solution.py:312
  40.2 0.3 shard_map.33
  40.5 0.0 collective-permute-done.4.gxa_ref
  40.5 0.6 %collective-permute-done.5.gxb_ref = f32[240,128]{1,0:T(8,128)S(1)} collective-permute-done((f32[240,128]{1,0:T(8,128)S(1)}, f32[240,128]{1,0:T(8,128)S(1)}, u32[]{:S(2)}, u32[]{:S(2)}) %collective-permute-start.5) | collective-permute-done | bytes 122912 | tf_op jit(solution)/shard_map/ppermute | solution.py:312
  41.1 1.6 %shard_map.34 = f32[16,16,16,128]{3,2,1,0:T(8,128)} custom-call(f32[16,16,16,128]{3,2,1,0:T(8,128)} %bitcast.7, f32[240,128]{1,0:T(8,128)S(1)} %collective-permute-done.4.gxa_ref, f32[240,128]{1,0:T(8,128)S(1)} %collective-permute-done.5.gxb_ref, f32[16,16,128]{2,1,0:T(8,128)S(1)} %get-tuple-element.55.mxa_ref, ...), custom_call_target="tpu_custom_call", output_to_operand_aliasing={{}: (0, {})} | custom-call | bytes 1048576 | tf_op jit(solution)/shard_map/pallas_call | solution.py:370
Async XLA Ops:
  0.0 15.2 %copy-start.2 = (s32[1,1,8,16]{3,2,1,0:T(8,128)S(1)}, s32[1,1,8,16]{3,2,1,0:T(8,128)}, u32[]{:S(2)}) copy-start(s32[1,1,8,16]{3,2,1,0:T(8,128)} %param.3) | copy-start | bytes 1540
  2.0 18.2 %collective-permute-start = (f32[248,128]{1,0:T(8,128)}, f32[248,128]{1,0:T(8,128)S(1)}, u32[]{:S(2)}, u32[]{:S(2)}) collective-permute-start(f32[248,128]{1,0:T(8,128)} %get-tuple-element.40), channel_id=1, source_target_pairs={{0,8},{8,0},{16,24},{24,16},{32,40},{40,32},{48,56},{56,48},{64,72... | collective-permute-start | bytes 380936 | tf_op jit(solution)/shard_map/ppermute | solution.py:312
  2.1 18.1 %collective-permute-start.1 = (f32[248,128]{1,0:T(8,128)}, f32[248,128]{1,0:T(8,128)S(1)}, u32[]{:S(2)}, u32[]{:S(2)}) collective-permute-start(f32[248,128]{1,0:T(8,128)} %get-tuple-element.41), channel_id=1, source_target_pairs={{8,16},{16,8},{24,32},{32,24},{40,48},{48,40},{56,64},{64,56},{72,... | collective-permute-start | bytes 380936 | tf_op jit(solution)/shard_map/ppermute | solution.py:312
  9.3 19.8 %collective-permute-start.2 = (f32[248,128]{1,0:T(8,128)}, f32[248,128]{1,0:T(8,128)S(1)}, u32[]{:S(2)}, u32[]{:S(2)}) collective-permute-start(f32[248,128]{1,0:T(8,128)} %get-tuple-element.46), channel_id=1, source_target_pairs={{0,1},{1,0},{2,3},{3,2},{4,5},{5,4},{6,7},{7,6},{8,9},{9,8},{10,11... | collective-permute-start | bytes 380936 | tf_op jit(solution)/shard_map/ppermute | solution.py:312
  13.8 15.3 %collective-permute-start.3 = (f32[248,128]{1,0:T(8,128)}, f32[248,128]{1,0:T(8,128)S(1)}, u32[]{:S(2)}, u32[]{:S(2)}) collective-permute-start(f32[248,128]{1,0:T(8,128)} %get-tuple-element.47), channel_id=1, source_target_pairs={{1,2},{2,1},{3,4},{4,3},{5,6},{6,5},{7,0},{0,7},{9,10},{10,9},{11,... | collective-permute-start | bytes 380936 | tf_op jit(solution)/shard_map/ppermute | solution.py:312
  15.2 1.6 %copy-start = (f32[16,16,16,128]{3,2,1,0:T(8,128)S(1)}, f32[16,16,16,128]{3,2,1,0:T(8,128)}, u32[]{:S(2)}) copy-start(f32[16,16,16,128]{3,2,1,0:T(8,128)} %field_ref.1) | copy-start | bytes 6291460
  16.8 13.3 %copy-start.1 = (f32[16,16,16,128]{3,2,1,0:T(8,128)S(1)}, f32[16,16,16,128]{3,2,1,0:T(8,128)}, u32[]{:S(2)}) copy-start(f32[16,16,16,128]{3,2,1,0:T(8,128)} %field_ref.1) | copy-start | bytes 6291460
  20.9 14.1 %collective-permute-start.6 = (f32[240,128]{1,0:T(8,128)S(1)}, f32[240,128]{1,0:T(8,128)S(1)}, u32[]{:S(2)}, u32[]{:S(2)}) collective-permute-start(f32[240,128]{1,0:T(8,128)S(1)} %get-tuple-element.59), channel_id=1, source_target_pairs={{0,1},{1,0},{2,3},{3,2},{4,5},{5,4},{6,7},{7,6},{8,9},{9,8},{10,11... | collective-permute-start | bytes 368648 | tf_op jit(solution)/shard_map/ppermute | solution.py:312
  26.4 13.8 %collective-permute-start.7 = (f32[240,128]{1,0:T(8,128)S(1)}, f32[240,128]{1,0:T(8,128)S(1)}, u32[]{:S(2)}, u32[]{:S(2)}) collective-permute-start(f32[240,128]{1,0:T(8,128)S(1)} %get-tuple-element.60), channel_id=1, source_target_pairs={{1,2},{2,1},{3,4},{4,3},{5,6},{6,5},{7,0},{0,7},{9,10},{10,9},{11,... | collective-permute-start | bytes 368648 | tf_op jit(solution)/shard_map/ppermute | solution.py:312
  29.7 10.8 %collective-permute-start.4 = (f32[240,128]{1,0:T(8,128)S(1)}, f32[240,128]{1,0:T(8,128)S(1)}, u32[]{:S(2)}, u32[]{:S(2)}) collective-permute-start(f32[240,128]{1,0:T(8,128)S(1)} %get-tuple-element.53), channel_id=1, source_target_pairs={{0,8},{8,0},{16,24},{24,16},{32,40},{40,32},{48,56},{56,48},{64,72... | collective-permute-start | bytes 368648 | tf_op jit(solution)/shard_map/ppermute | solution.py:312
  29.8 11.3 %collective-permute-start.5 = (f32[240,128]{1,0:T(8,128)S(1)}, f32[240,128]{1,0:T(8,128)S(1)}, u32[]{:S(2)}, u32[]{:S(2)}) collective-permute-start(f32[240,128]{1,0:T(8,128)S(1)} %get-tuple-element.54), channel_id=1, source_target_pairs={{8,16},{16,8},{24,32},{32,24},{40,48},{48,40},{56,64},{64,56},{72,... | collective-permute-start | bytes 368648 | tf_op jit(solution)/shard_map/ppermute | solution.py:312
